TPU v7x, 256 devices: a whole 4x4x8 slice. The times are simulated.
256 devices in a mesh: group: 4 (over y_hi, core), dp: 64 (over z, y_lo, x).
Axes of the slice: x: 4, y: 4 (y_hi: 2, y_lo: 2; y = y_hi * 2 + y_lo), z: 8, core: 2. Of those that a mesh axis runs over, the one named last changes fastest.
Arguments:
- gelu_pooled_inner: bfloat16 [14336, 12288], P(('group', 'dp')), may hold values from -1.5 to 1.5
- frozen_pooled_trunk_result: bfloat16 [14336, 3072], P(('group', 'dp')), may hold values from -62 to 62
- narrowing_weight: bfloat16 [12288, 16], replicated, may hold values from -0.0546875 to 0.0546875
- widening_weight: bfloat16 [16, 3072], replicated, may hold values from -1.5 to 1.5
- closing_standardize_multiplier: float32 [3072], replicated, may hold values from 0.5 to 2
- closing_standardize_addend: float32 [3072], replicated, may hold values from -3 to 3
- closing_projection_weight: bfloat16 [3072, 1024], replicated, may hold values from -0.109375 to 0.109375
- sentence_encodings: bfloat16 [14336, 1024], P(('group', 'dp')), may hold values from -62 to 62
- logged_sharpening: float32 [1], replicated, may hold values from 2 to 2.6
- sigmoid_threshold_term: float32 [1], replicated, may hold values from -4 to -2
Outputs:
- sphere_visual_derivative: float32 [14336, 1024], P(('group', 'dp'))
- adapter_down_gradient: float32 [12288, 16], replicated
- adapter_up_gradient: float32 [16, 3072], replicated
All inputs are finite; a program needn't handle non-finite values.
Results may differ from a plain program's by a relative error of at most 0.0085.
Values may be sent and summed in bfloat16 or wider, within the bound.
A program may use at most 128 MiB of HBM per device.

v0:
```python
import jax
import jax.numpy as jnp
from jax import lax
from jax.sharding import PartitionSpec as P

norm_eps = 1e-06


def visual_encoder_evaluate(
    gelu_pooled_inner,
    frozen_pooled_trunk_result,
    narrowing_weight,
    widening_weight,
    closing_standardize_multiplier,
    closing_standardize_addend,
    closing_projection_weight,
):
    lowdim_compressed = jnp.dot(
        gelu_pooled_inner, narrowing_weight, preferred_element_type=jnp.float32
    ).astype(jnp.bfloat16)
    trailing_result = frozen_pooled_trunk_result.astype(jnp.float32) + jnp.dot(
        lowdim_compressed, widening_weight, preferred_element_type=jnp.float32
    )
    centred = trailing_result - jnp.mean(trailing_result, axis=1, keepdims=True)
    reciprocal_spread = lax.rsqrt(jnp.mean(centred * centred, axis=1, keepdims=True) + norm_eps)
    standardized_traits = centred * reciprocal_spread
    head_in = (
        standardized_traits * closing_standardize_multiplier + closing_standardize_addend
    ).astype(jnp.bfloat16)
    embedding = jnp.dot(head_in, closing_projection_weight, preferred_element_type=jnp.float32)
    reciprocal_magnitude = lax.rsqrt(
        jnp.sum(embedding * embedding, axis=1, keepdims=True) + norm_eps
    )
    return (
        lowdim_compressed,
        standardized_traits,
        reciprocal_spread,
        embedding * reciprocal_magnitude,
        reciprocal_magnitude,
    )


def unit_rows(sentence_encodings):
    values = sentence_encodings.astype(jnp.float32)
    return (values * lax.rsqrt(jnp.sum(values * values, axis=1, keepdims=True) + norm_eps)).astype(
        jnp.bfloat16
    )


def duo_costs(sentence_subset, photo_batch_part, photo_total, steepness_number, beginning_position):
    cosine_values = lax.dot_general(
        sentence_subset,
        photo_batch_part,
        (((1,), (1,)), ((), ())),
        preferred_element_type=jnp.float32,
    )
    affinity_entries = steepness_number * cosine_values + beginning_position
    text_ids = lax.iota(jnp.int32, sentence_subset.shape[0])
    positive_sign_targets = (text_ids[:, None] == photo_total[None, :]).astype(jnp.float32)
    penalty_coefficients = (
        steepness_number * (jax.nn.sigmoid(affinity_entries) - positive_sign_targets)
    ).astype(jnp.bfloat16)
    return lax.dot_general(
        penalty_coefficients,
        sentence_subset,
        (((0,), (0,)), ((), ())),
        preferred_element_type=jnp.float32,
    )


def body(
    gelu_pooled_inner,
    frozen_pooled_trunk_result,
    narrowing_weight,
    widening_weight,
    closing_standardize_multiplier,
    closing_standardize_addend,
    closing_projection_weight,
    sentence_encodings,
    logged_sharpening,
    sigmoid_threshold_term,
):
    own_rows = gelu_pooled_inner.shape[0]
    (
        lowdim_compressed,
        standardized_traits,
        reciprocal_spread,
        sphere_visual,
        reciprocal_magnitude,
    ) = visual_encoder_evaluate(
        gelu_pooled_inner,
        frozen_pooled_trunk_result,
        narrowing_weight,
        widening_weight,
        closing_standardize_multiplier,
        closing_standardize_addend,
        closing_projection_weight,
    )
    photo_batch_part = sphere_visual.astype(jnp.bfloat16)
    text_rows = unit_rows(sentence_encodings)
    steepness_number = jnp.exp(logged_sharpening[0])
    beginning_position = sigmoid_threshold_term[0]
    col_count = lax.axis_size("dp")
    row_index = lax.axis_index("group")
    col_index = lax.axis_index("dp")
    own_ids = (row_index * col_count + col_index) * own_rows + lax.iota(jnp.int32, own_rows)
    sphere_visual_derivative = duo_costs(
        lax.all_gather(text_rows, ("group", "dp"), axis=0, tiled=True),
        photo_batch_part,
        own_ids,
        steepness_number,
        beginning_position,
    )
    projection = jnp.sum(sphere_visual * sphere_visual_derivative, axis=1, keepdims=True)
    embed_grad = (
        reciprocal_magnitude * (sphere_visual_derivative - sphere_visual * projection)
    ).astype(jnp.bfloat16)
    head_grad = lax.dot_general(
        embed_grad,
        closing_projection_weight,
        (((1,), (1,)), ((), ())),
        preferred_element_type=jnp.float32,
    )
    scaled = head_grad * closing_standardize_multiplier
    trailing_derivative = reciprocal_spread * (
        scaled
        - jnp.mean(scaled, axis=1, keepdims=True)
        - standardized_traits * jnp.mean(scaled * standardized_traits, axis=1, keepdims=True)
    )
    trailing_derivative = trailing_derivative.astype(jnp.bfloat16)
    up_part = lax.dot_general(
        lowdim_compressed,
        trailing_derivative,
        (((0,), (0,)), ((), ())),
        preferred_element_type=jnp.float32,
    )
    lowdim_reverse_pass = lax.dot_general(
        trailing_derivative,
        widening_weight,
        (((1,), (1,)), ((), ())),
        preferred_element_type=jnp.float32,
    ).astype(jnp.bfloat16)
    down_part = lax.dot_general(
        gelu_pooled_inner,
        lowdim_reverse_pass,
        (((0,), (0,)), ((), ())),
        preferred_element_type=jnp.float32,
    )
    down_grad, up_grad = lax.psum((down_part, up_part), ("group", "dp"))
    return (sphere_visual_derivative, down_grad, up_grad)


def solution(mesh):
    return jax.shard_map(
        body,
        mesh=mesh,
        in_specs=(
            P(("group", "dp"), None),
            P(("group", "dp"), None),
            P(),
            P(),
            P(),
            P(),
            P(),
            P(("group", "dp"), None),
            P(),
            P(),
        ),
        out_specs=(P(("group", "dp"), None), P(), P()),
        check_vma=False,
    )
```

profile of v0, /device:TPU:1, one launch (start us, length us, event | category | flops | bytes accessed | tf_op | source)
XLA Modules:
  0.0 1065.7 jit_solution(3017418578877380673)
XLA Ops:
  7.2 0.0 copy-start
  7.2 0.0 copy-start.3
  7.2 0.0 copy-start.4
  7.2 0.0 all-gather.2.cloned.1.call-start
  7.2 1.1 fusion.14
  8.4 1.6 fusion.15
  10.0 0.0 all-gather.2.cloned.1.call-update
  10.0 0.0 all-reduce.3.cloned.1.call-start
  11.4 0.0 copy-done
  11.5 1.5 convolution_convert_fusion.1
  12.9 1.4 fusion.22
  14.4 0.2 multiply_reduce_fusion.1
  14.6 0.0 copy-done.3
  14.6 0.0 copy-done.4
  14.6 4.1 multiply_reduce_fusion.3
  18.8 745.1 %all-gather.2.cloned.1.call-done = bf16[14336,1024]{1,0:T(8,128)(2,1)} async-done(((bf16[56,1024]{1,0:T(8,128)(2,1)}), bf16[14336,1024]{1,0:T(8,128)(2,1)}) %all-gather.2.cloned.1.call-update) | async-done | bytes 29360144 | tf_op jit(solution)/shard_map/all_gather | solution.py:108
  763.9 29.0 %multiply_reduce_fusion.2 = (f32[56]{0:T(128)S(1)}, f32[56,1024]{1,0:T(8,128)S(1)}) fusion(f32[56,1024]{1,0:T(8,128)S(1)} %get-tuple-element.10, f32[56]{0:T(128)S(1)} %add_rsqrt_fusion, bf16[14336,1024]{1,0:T(8,128)(2,1)} %all-gather.2.cloned.1.call-done, s32[56]{0:T(128)S(1)} %iota_add_fusion, f32[]{:T(128)} %bitcast.17, f32[]{:T(128)} %bitcast), kind=kOutput, calls=%fused_computation.31 | convolution fusion | flops 3296649216 | bytes 29819560 | tf_op jit(solution)/shard_map/dot_general | solution.py:63
  792.9 0.0 copy-start.2
  792.9 0.0 copy-start.1
  792.9 5.1 fusion.21
  798.0 0.0 copy-done.2
  798.0 0.2 multiply_convert_fusion
  798.2 0.9 fusion.23
  799.1 0.0 copy-done.1
  799.1 1.6 convolution_bitcast_fusion
  800.7 0.0 all-reduce.3.cloned.1.call-update
  800.8 254.4 %all-reduce.3.cloned.1.call-done = (f32[12288,16]{0,1:T(8,128)}, f32[16,3072]{1,0:T(8,128)}) async-done(((f32[12288,16]{0,1:T(8,128)}, f32[16,3072]{1,0:T(8,128)}), (f32[12288,16]{0,1:T(8,128)}, f32[16,3072]{1,0:T(8,128)})) %all-reduce.3.cloned.1.call-update) | async-done | bytes 983056 | tf_op jit(solution)/shard_map/psum | solution.py:149
  1055.1 2.1 copy.17
  1057.2 1.6 copy.18
  (6 shorter events, 0.0 us)
Async XLA Ops:
  7.2 4.3 copy-start
  7.2 7.4 copy-start.3
  7.2 7.4 copy-start.4
  7.2 756.7 %all-gather.2.cloned.1.call-start = ((), (), s32[]{:S(2)}) async-start(), calls=%async_computation | async-start | bytes 29474816 | tf_op jit(solution)/shard_map/all_gather | solution.py:108
  10.0 1045.1 %all-reduce.3.cloned.1.call-start = ((), (), s32[]{:S(2)}) async-start(), calls=%async_computation.1 | async-start | bytes 1966080 | tf_op jit(solution)/shard_map/psum | solution.py:149
  792.9 5.1 copy-start.2
  792.9 6.2 copy-start.1
Sparse Core Ops, SparseCore 0:
  10.5 753.3 all-gather.1
  800.9 254.2 all-reduce.2
where the time goes:
time: 1070 us
  waiting for transfers between devices  1000 us (93%)
  matrix products  43.6 us (4%)
  between operations  15.5 us (1%)
    all_gather x1, waiting for transfers between devices, body(): lax.all_gather(text_rows, ('group', 'dp'), axis=0, tiled=True)  745 us
    psum x1, waiting for transfers between devices, body(): down_grad, up_grad = lax.psum((down_part, up_part), ('group', 'dp'))  254 us
    dot_general x1, matrix products, duo_costs(): lax.dot_general(penalty_coefficients, sentence_subset, (((0,), (0,)), (()...  29 us
  transfers between devices with their start and end apart: 2, of which 2 were waited for; matrix products, arithmetic and copies ran while one was open for 1% of the time, Pallas kernels for 0%

commit v1 on v0

v1 whole, which is shorter than its diff:
```python
import jax
import jax.numpy as jnp
from jax import lax
from jax.experimental import pallas as pl
from jax.experimental.pallas import tpu as pltpu
from jax.sharding import PartitionSpec as P

norm_eps = 1e-06
MESH = pl.DeviceIdType.MESH
BF16, F32 = jnp.bfloat16, jnp.float32

X, YL, YH, Z = 4, 2, 2, 8
Y = YL * YH
ROWS = 56
PAIR = 2 * ROWS
E, DEPTH, INNER, RANK = 1024, 3072, 12288, 16
QUARTER = E // 4
IMAGES = X * ROWS
TEXTS = Y * PAIR
PLANE = X * Y
CUT = 512
UP, DOWN = Z // 2, Z // 2 - 1


def remote(src, dst, send_sem, recv_sem, device):
    return pltpu.make_async_remote_copy(
        src_ref=src,
        dst_ref=dst,
        send_sem=send_sem,
        recv_sem=recv_sem,
        device_id=device,
        device_id_type=MESH,
    )


def nt(a, b):
    return lax.dot_general(a, b, (((1,), (1,)), ((), ())), preferred_element_type=F32)


def nn(a, b):
    return lax.dot_general(a, b, (((1,), (0,)), ((), ())), preferred_element_type=F32)


def kernel(
    inner_h,
    trunk_h,
    narrow_h,
    widen_h,
    gain_h,
    bias_h,
    head_h,
    text_h,
    sharp_ref,
    shift_ref,
    dv_h,
    grad_h,
    inner,
    trunk,
    narrow,
    widen,
    gain,
    bias,
    head,
    raw,
    texts,
    image_wire,
    images,
    dv,
    dv_send,
    dv_recv,
    dv_own,
    unit,
    normed,
    grads,
    pair_send,
    pair_recv,
    half,
    plane_send,
    plane_recv,
    ring_recv,
    final,
    load_sem,
    raw_send,
    raw_recv,
    pz_send,
    pz_recv,
    py_send,
    py_recv,
    qy_send,
    qy_recv,
    qz_send,
    qz_recv,
    sib_send,
    sib_recv,
    img_send,
    img_recv,
    rs_send,
    rs_recv,
    pair_ssem,
    pair_rsem,
    plane_ssem,
    plane_rsem,
    ring_ssem,
    ring_rsem,
    back_ssem,
    back_rsem,
    last_ssem,
    last_rsem,
    out_sem,
):
    g, d = lax.axis_index("group"), lax.axis_index("dp")
    c, yh = lax.rem(g, 2), lax.div(g, 2)
    z, yl, x = lax.div(d, YL * X), lax.rem(lax.div(d, X), YL), lax.rem(d, X)
    y = yh * YL + yl
    k = y * X + x

    def device(xx, yy, zz, cc):
        return (
            lax.div(yy, YL) * 2 + cc,
            zz * (YL * X) + lax.rem(yy, YL) * X + xx,
        )

    sibling = device(x, y, z, 1 - c)
    above = device(x, y, lax.rem(z + 1, Z), c)
    below = device(x, y, lax.rem(z + Z - 1, Z), c)

    def at_y(o):
        return lax.rem(y + o, Y)

    def at_x(o):
        return lax.rem(x + o, X)

    def at_z(o):
        return lax.rem(z + o + Z, Z)

    def at_k(o):
        return lax.rem(k + o, PLANE)

    def plane_device(kk):
        return device(lax.rem(kk, X), lax.div(kk, X), z, c)

    loads = [
        pltpu.make_async_copy(text_h, raw.at[c], load_sem.at[0]),
        pltpu.make_async_copy(inner_h, inner, load_sem.at[1]),
        pltpu.make_async_copy(narrow_h, narrow, load_sem.at[2]),
        pltpu.make_async_copy(widen_h, widen, load_sem.at[3]),
        pltpu.make_async_copy(trunk_h, trunk, load_sem.at[4]),
        pltpu.make_async_copy(gain_h, gain, load_sem.at[5]),
        pltpu.make_async_copy(bias_h, bias, load_sem.at[6]),
        pltpu.make_async_copy(head_h, head, load_sem.at[7]),
    ]
    barrier = pltpu.get_barrier_semaphore()
    pl.semaphore_signal(barrier, inc=1, device_id=sibling, device_id_type=MESH)

    @pl.loop(1, PLANE)
    def _(o):
        pl.semaphore_signal(barrier, inc=1, device_id=plane_device(at_k(o)), device_id_type=MESH)

    @pl.loop(1, Z)
    def _(o):
        pl.semaphore_signal(barrier, inc=1, device_id=device(x, y, at_z(o), c), device_id_type=MESH)

    for load in loads:
        load.start()
    pl.semaphore_wait(barrier, 1 + (PLANE - 1) + (Z - 1))

    raw_copy = remote(text_h, raw.at[c], raw_send, raw_recv, sibling)
    raw_copy.start()
    loads[0].wait()
    raw_copy.wait_recv()

    halves = []
    for i in range(2):
        whole = raw[i].astype(F32)
        scale = lax.rsqrt(jnp.sum(whole * whole, axis=1, keepdims=True) + norm_eps)
        part = raw[i, :, pl.ds(pl.multiple_of(c * (E // 2), E // 2), E // 2)].astype(F32)
        halves.append(part * scale)
    block = jnp.concatenate(halves, axis=0).astype(BF16)
    texts[c, z, 0, y] = block[:, :QUARTER]
    texts[c, z, 1, y] = block[:, QUARTER:]

    def piece0_up(zz, hop):
        ref = texts.at[c, zz, 0, y]
        return remote(ref, ref, pz_send.at[hop], pz_recv.at[zz], above)

    def piece0_down(zz, hop):
        ref = texts.at[c, zz, 0, y]
        return remote(ref, ref, pz_send.at[UP + hop], pz_recv.at[zz], below)

    def piece0_y(zz, o):
        ref = texts.at[c, zz, 0, y]
        return remote(ref, ref, py_send.at[zz, o - 1], py_recv.at[zz, y], device(x, at_y(o), z, c))

    def piece0_y_wait(zz, o):
        ref = texts.at[c, zz, 0, at_y(o)]
        remote(ref, ref, py_send.at[0, 0], py_recv.at[zz, at_y(o)], sibling).wait_recv()

    def piece1_y(o):
        ref = texts.at[c, z, 1, y]
        return remote(ref, ref, qy_send.at[o - 1], qy_recv.at[y], device(x, at_y(o), z, c))

    def piece1_y_wait(o):
        ref = texts.at[c, z, 1, at_y(o)]
        remote(ref, ref, qy_send.at[0], qy_recv.at[at_y(o)], sibling).wait_recv()

    def piece1_up(zz, hop):
        ref = texts.at[c, zz, 1]
        return remote(ref, ref, qz_send.at[hop], qz_recv.at[zz], above)

    def piece1_down(zz, hop):
        ref = texts.at[c, zz, 1]
        return remote(ref, ref, qz_send.at[UP + hop], qz_recv.at[zz], below)

    def across(zz):
        ref = texts.at[c, zz]
        return remote(ref, ref, sib_send.at[zz], sib_recv.at[zz], sibling)

    def spread0(zz):
        @pl.loop(1, Y)
        def _(o):
            piece0_y(zz, o).start()

    @pl.loop(1, Y)
    def _(o):
        piece1_y(o).start()

    piece0_up(z, 0).start()
    piece0_down(z, 0).start()
    spread0(z)

    def pass0(distance):
        zz = at_z(-distance)
        piece0_up(zz, 0).wait_recv()
        if distance < UP:
            piece0_up(zz, distance).start()
        spread0(zz)
        if distance <= DOWN:
            zz = at_z(distance)
            piece0_down(zz, 0).wait_recv()
            if distance < DOWN:
                piece0_down(zz, distance).start()
            spread0(zz)

    loads[1].wait()
    loads[2].wait()
    step = INNER // 4
    low = jnp.zeros((ROWS, RANK), F32)
    for i in range(4):
        cols = pl.ds(i * step, step)
        low = low + nt(inner[:, cols], narrow[:, cols])
    low = low.astype(BF16)

    @pl.loop(1, Y)
    def _(o):
        piece1_y_wait(o)

    piece1_up(z, 0).start()
    piece1_down(z, 0).start()
    pass0(1)

    loads[3].wait()
    loads[4].wait()
    loads[5].wait()
    loads[6].wait()
    section = trunk[...].astype(F32) + nn(low, widen[...])
    centred = section - jnp.mean(section, axis=1, keepdims=True)
    inv_std = lax.rsqrt(jnp.mean(centred * centred, axis=1, keepdims=True) + norm_eps)
    spread = centred * inv_std
    normed[...] = spread
    head_in = (spread * gain[...] + bias[...]).astype(BF16)
    pass0(2)
    loads[7].wait()
    embedding = nn(head_in, head[...])
    inv_len = lax.rsqrt(jnp.sum(embedding * embedding, axis=1, keepdims=True) + norm_eps)
    embedding = embedding * inv_len
    unit[...] = embedding

    def to_wire(ref, quarters):
        ref[:, :QUARTER] = jnp.concatenate([quarters[0], quarters[2]], axis=0).astype(BF16)
        ref[:, QUARTER:] = jnp.concatenate([quarters[1], quarters[3]], axis=0).astype(BF16)

    def from_wire(ref):
        left = ref[:, :QUARTER].astype(F32)
        right = ref[:, QUARTER:].astype(F32)
        return [left[:ROWS], right[:ROWS], left[ROWS:], right[ROWS:]]

    to_wire(image_wire.at[x], [embedding[:, q * QUARTER : (q + 1) * QUARTER] for q in range(4)])

    def send_images(o):
        ref = image_wire.at[x]
        return remote(ref, ref, img_send.at[o - 1], img_recv.at[x], device(at_x(o), y, z, c))

    @pl.loop(1, X)
    def _(o):
        send_images(o).start()

    pass0(3)
    pass0(4)

    def prepare(s):
        zz = at_z(lax.rem(s, 2) * -(lax.div(s + 1, 2)) + (1 - lax.rem(s, 2)) * lax.div(s, 2))

        @pl.when(lax.rem(s, 2) == 1)
        def _():
            distance = lax.div(s + 1, 2)
            piece1_up(zz, 0).wait_recv()

            @pl.when(distance < UP)
            def _():
                piece1_up(zz, distance).start()

        @pl.when((lax.rem(s, 2) == 0) & (s > 0))
        def _():
            distance = lax.div(s, 2)
            piece1_down(zz, 0).wait_recv()

            @pl.when(distance < DOWN)
            def _():
                piece1_down(zz, distance).start()

        @pl.loop(1, Y)
        def _(o):
            piece0_y_wait(zz, o)

        across(zz).start()

    prepare(jnp.int32(0))

    @pl.loop(1, X)
    def _(o):
        ref = image_wire.at[at_x(o)]
        remote(ref, ref, img_send.at[0], img_recv.at[at_x(o)], sibling).wait_recv()

    wires = [from_wire(image_wire.at[i]) for i in range(X)]
    for q in range(4):
        images[q] = jnp.concatenate([wire[q] for wire in wires], axis=0).astype(BF16)

    sharp = jnp.exp(jnp.full((1, TEXTS), sharp_ref[0], F32))
    shift = jnp.full((1, TEXTS), shift_ref[0], F32)

    dv[...] = jnp.zeros_like(dv)

    @pl.loop(0, Z)
    def _(s):
        @pl.when(s < Z - 1)
        def _():
            prepare(s + 1)

        zz = at_z(lax.rem(s, 2) * -(lax.div(s + 1, 2)) + (1 - lax.rem(s, 2)) * lax.div(s, 2))
        ref = texts.at[1 - c, zz]
        remote(ref, ref, sib_send.at[0], sib_recv.at[zz], sibling).wait_recv()
        parts = [texts[q // 2, zz, q % 2].reshape(TEXTS, QUARTER) for q in range(4)]
        cosine = nt(images[0], parts[0])
        for q in range(1, 4):
            cosine = cosine + nt(images[q], parts[q])
        row = lax.broadcasted_iota(jnp.int32, (IMAGES, TEXTS), 0) - x * ROWS
        col = lax.broadcasted_iota(jnp.int32, (IMAGES, TEXTS), 1) - y * PAIR - c * ROWS
        same = (row == col) & (row >= 0) & (row < ROWS) & (s == 0)
        weights = sharp * (jax.nn.sigmoid(sharp * cosine + shift) - jnp.where(same, 1.0, 0.0))
        weights = weights.astype(BF16)
        for q in range(4):
            dv[q] += nn(weights, parts[q])

    def send_sum(o):
        return remote(
            dv_send.at[o - 1],
            dv_recv.at[x],
            rs_send.at[o - 1],
            rs_recv.at[x],
            device(at_x(o), y, z, c),
        )

    def rows_of(xx):
        return pl.ds(pl.multiple_of(xx * ROWS, 8), ROWS)

    for o in range(1, X):
        to_wire(dv_send.at[o - 1], [dv[q, rows_of(at_x(o))] for q in range(4)])
        send_sum(o).start()
    total = [dv[q, rows_of(x)] for q in range(4)]
    for o in range(1, X):
        ref = dv_recv.at[at_x(o)]
        remote(ref, ref, rs_send.at[0], rs_recv.at[at_x(o)], sibling).wait_recv()
        total = [a + b for a, b in zip(total, from_wire(ref))]
    derivative = jnp.concatenate(total, axis=1)
    dv_own[...] = derivative
    dv_copy = pltpu.make_async_copy(dv_own, dv_h, out_sem.at[0])
    dv_copy.start()

    embedding = unit[...]
    along = jnp.sum(embedding * derivative, axis=1, keepdims=True)
    embed_grad = (inv_len * (derivative - embedding * along)).astype(BF16)
    scaled = nt(embed_grad, head[...]) * gain[...]
    spread = normed[...]
    section_grad = inv_std * (
        scaled
        - jnp.mean(scaled, axis=1, keepdims=True)
        - spread * jnp.mean(scaled * spread, axis=1, keepdims=True)
    )
    section_grad = section_grad.astype(BF16)
    back = nt(widen[...], section_grad).astype(BF16)
    up = lax.dot_general(low, section_grad, (((0,), (0,)), ((), ())), preferred_element_type=F32)
    n_down, n_up = INNER // CUT, DEPTH // CUT
    for i in range(n_down):
        grads[i // PLANE, i % PLANE] = nn(back, inner[:, pl.ds(i * CUT, CUT)])
    for i in range(n_up):
        j = n_down + i
        grads[j // PLANE, j % PLANE] = up[:, i * CUT : (i + 1) * CUT]
    for j in range(n_down + n_up, 2 * PLANE):
        grads[j // PLANE, j % PLANE] = jnp.zeros((RANK, CUT), F32)

    pair_send[...] = grads[1 - c].astype(BF16)
    pair_copy = remote(pair_send, pair_recv, pair_ssem, pair_rsem, sibling)
    pair_copy.start()
    pair_copy.wait_recv()
    half[...] = grads[c] + pair_recv[...].astype(F32)
    plane_send[...] = half[...].astype(BF16)

    def plane_copy(o):
        kk = at_k(o)
        return remote(
            plane_send.at[kk],
            plane_recv.at[k],
            plane_ssem.at[o - 1],
            plane_rsem.at[k],
            plane_device(kk),
        )

    @pl.loop(1, PLANE)
    def _(o):
        plane_copy(o).start()

    plane_recv[k] = plane_send[k]

    @pl.loop(1, PLANE)
    def _(o):
        ref = plane_recv.at[at_k(o)]
        remote(ref, ref, plane_ssem.at[0], plane_rsem.at[at_k(o)], sibling).wait_recv()

    ring_recv[z] = jnp.sum(plane_recv[...].astype(F32), axis=0).astype(BF16)

    def ring_copy(o):
        ref = ring_recv.at[z]
        return remote(ref, ref, ring_ssem.at[o - 1], ring_rsem.at[z], device(x, y, at_z(o), c))

    @pl.loop(1, Z)
    def _(o):
        ring_copy(o).start()

    @pl.loop(1, Z)
    def _(o):
        ref = ring_recv.at[at_z(o)]
        remote(ref, ref, ring_ssem.at[0], ring_rsem.at[at_z(o)], sibling).wait_recv()

    final[c, k] = jnp.sum(ring_recv[...].astype(F32), axis=0).astype(BF16)

    def back_copy(o):
        ref = final.at[c, k]
        return remote(ref, ref, back_ssem.at[o - 1], back_rsem.at[k], plane_device(at_k(o)))

    def last_copy(kk):
        ref = final.at[c, kk]
        return remote(ref, ref, last_ssem.at[kk], last_rsem.at[kk], sibling)

    @pl.loop(1, PLANE)
    def _(o):
        back_copy(o).start()

    last_copy(k).start()

    @pl.loop(1, PLANE)
    def _(o):
        kk = at_k(o)
        ref = final.at[c, kk]
        remote(ref, ref, back_ssem.at[0], back_rsem.at[kk], sibling).wait_recv()
        last_copy(kk).start()

    @pl.loop(0, PLANE)
    def _(kk):
        ref = final.at[1 - c, kk]
        remote(ref, ref, last_ssem.at[0], last_rsem.at[kk], sibling).wait_recv()

    grad_copy = pltpu.make_async_copy(final, grad_h, out_sem.at[1])
    grad_copy.start()

    raw_copy.wait_send()
    for hop in range(UP):
        piece0_up(z, hop).wait_send()
        piece1_up(z, hop).wait_send()
    for hop in range(DOWN):
        piece0_down(z, hop).wait_send()
        piece1_down(z, hop).wait_send()

    @pl.loop(1, Y)
    def _(o):
        piece1_y(o).wait_send()

        @pl.loop(0, Z)
        def _(zz):
            piece0_y(zz, o).wait_send()

    @pl.loop(0, Z)
    def _(zz):
        across(zz).wait_send()

    @pl.loop(1, X)
    def _(o):
        send_images(o).wait_send()
        send_sum(o).wait_send()

    pair_copy.wait_send()

    @pl.loop(1, PLANE)
    def _(o):
        plane_copy(o).wait_send()
        back_copy(o).wait_send()

    @pl.loop(1, Z)
    def _(o):
        ring_copy(o).wait_send()

    @pl.loop(0, PLANE)
    def _(kk):
        last_copy(kk).wait_send()

    dv_copy.wait()
    grad_copy.wait()


def body(
    gelu_pooled_inner,
    frozen_pooled_trunk_result,
    narrowing_weight,
    widening_weight,
    closing_standardize_multiplier,
    closing_standardize_addend,
    closing_projection_weight,
    sentence_encodings,
    logged_sharpening,
    sigmoid_threshold_term,
):
    anywhere = pl.BlockSpec(memory_space=pl.ANY)
    scalar = pl.BlockSpec(memory_space=pltpu.SMEM)
    dma = pltpu.SemaphoreType.DMA
    derivative, final = pl.pallas_call(
        kernel,
        out_shape=(
            jax.ShapeDtypeStruct((ROWS, E), F32),
            jax.ShapeDtypeStruct((2, PLANE, RANK, CUT), BF16),
        ),
        in_specs=[anywhere] * 8 + [scalar] * 2,
        out_specs=(anywhere, anywhere),
        scratch_shapes=[
            pltpu.VMEM((ROWS, INNER), BF16),
            pltpu.VMEM((ROWS, DEPTH), BF16),
            pltpu.VMEM((RANK, INNER), BF16),
            pltpu.VMEM((RANK, DEPTH), BF16),
            pltpu.VMEM((1, DEPTH), F32),
            pltpu.VMEM((1, DEPTH), F32),
            pltpu.VMEM((DEPTH, E), BF16),
            pltpu.VMEM((2, ROWS, E), BF16),
            pltpu.VMEM((2, Z, 2, Y, PAIR, QUARTER), BF16),
            pltpu.VMEM((X, PAIR, E // 2), BF16),
            pltpu.VMEM((4, IMAGES, QUARTER), BF16),
            pltpu.VMEM((4, IMAGES, QUARTER), F32),
            pltpu.VMEM((X - 1, PAIR, E // 2), BF16),
            pltpu.VMEM((X, PAIR, E // 2), BF16),
            pltpu.VMEM((ROWS, E), F32),
            pltpu.VMEM((ROWS, E), F32),
            pltpu.VMEM((ROWS, DEPTH), F32),
            pltpu.VMEM((2, PLANE, RANK, CUT), F32),
            pltpu.VMEM((PLANE, RANK, CUT), BF16),
            pltpu.VMEM((PLANE, RANK, CUT), BF16),
            pltpu.VMEM((PLANE, RANK, CUT), F32),
            pltpu.VMEM((PLANE, RANK, CUT), BF16),
            pltpu.VMEM((PLANE, RANK, CUT), BF16),
            pltpu.VMEM((Z, RANK, CUT), BF16),
            pltpu.VMEM((2, PLANE, RANK, CUT), BF16),
            dma((8,)),
            dma,
            dma,
            dma((UP + DOWN,)),
            dma((Z,)),
            dma((Z, Y - 1)),
            dma((Z, Y)),
            dma((Y - 1,)),
            dma((Y,)),
            dma((UP + DOWN,)),
            dma((Z,)),
            dma((Z,)),
            dma((Z,)),
            dma((X - 1,)),
            dma((X,)),
            dma((X - 1,)),
            dma((X,)),
            dma,
            dma,
            dma((PLANE - 1,)),
            dma((PLANE,)),
            dma((Z - 1,)),
            dma((Z,)),
            dma((PLANE - 1,)),
            dma((PLANE,)),
            dma((PLANE,)),
            dma((PLANE,)),
            dma((2,)),
        ],
        compiler_params=pltpu.CompilerParams(
            collective_id=0, has_side_effects=True, vmem_limit_bytes=48 * 1024 * 1024
        ),
    )(
        gelu_pooled_inner,
        frozen_pooled_trunk_result,
        narrowing_weight.T,
        widening_weight,
        closing_standardize_multiplier.reshape(1, DEPTH),
        closing_standardize_addend.reshape(1, DEPTH),
        closing_projection_weight,
        sentence_encodings,
        logged_sharpening,
        sigmoid_threshold_term,
    )
    pieces = final.reshape(2 * PLANE, RANK, CUT).transpose(1, 0, 2).reshape(RANK, -1).astype(F32)
    return derivative, pieces[:, :INNER].T, pieces[:, INNER : INNER + DEPTH]


def solution(mesh):
    rows = P(("group", "dp"), None)
    return jax.shard_map(
        body,
        mesh=mesh,
        in_specs=(rows, rows, P(), P(), P(), P(), P(), rows, P(), P()),
        out_specs=(rows, P(), P()),
        check_vma=False,
    )
```

time: 1070 us -> 100 us (0.09)
  waiting for transfers between devices: 1000 us -> 0 us
  Pallas kernels: 0 us -> 88.7 us
  matrix products: 43.6 us -> 0 us
  between operations: 15.5 us -> 1.96 us
    all_gather x1 -> x0, waiting for transfers between devices: 745 us -> none  [body(): lax.all_gather(text_rows, ('group', 'dp'), axis=0, tiled=True)]
    psum x1 -> x0, waiting for transfers between devices: 254 us -> none  [body(): down_grad, up_grad = lax.psum((down_part, up_part), ('group', 'dp'))]
    pallas_call x0 -> x1, Pallas kernels: none -> 88.7 us  [body(): pl.pallas_call(kernel, out_shape=(jax.ShapeDtypeStruct((ROWS, E), F32), j...]
    dot_general x7 -> x0, matrix products: 43.6 us -> none  [the longest x1 29 us: duo_costs(): lax.dot_general(penalty_coefficients, sentence_subset, (((0,), (0,)), (()...]
  transfers between devices with their start and end apart: 2 -> 0, of which waited for: 2 -> 0; matrix products, arithmetic and copies ran while one was open for 1% -> 0% of each run, Pallas kernels for 0% -> 0%
where the time goes in v1:
time: 100 us; the launch traced here: 99.7 us
  Pallas kernels  88.7 us (89%)
  local copies, waits for them, and re-layouts  8.9 us (9%)
  between operations  1.96 us (2%)
    pallas_call x1, Pallas kernels, body(): pl.pallas_call(kernel, out_shape=(jax.ShapeDtypeStruct((ROWS, E), F32), j...  88.7 us
    unnamed x15, local copies, waits for them, and re-layouts  7.2 us

profile of v1, /device:TPU:1, one launch (start us, length us, event | category | flops | bytes accessed | tf_op | source)
XLA Modules:
  0.0 99.7 jit_solution(14496136451601768816)
XLA Ops:
  1.9 0.0 copy-start
  1.9 1.3 %copy-done = bf16[56,12288]{1,0:T(8,128)(2,1)S(1)} copy-done((bf16[56,12288]{1,0:T(8,128)(2,1)S(1)}, bf16[56,12288]{1,0:T(8,128)(2,1)}, u32[]{:S(2)}) %copy-start) | copy-done | bytes 1376280
  3.3 0.0 copy-start.1
  3.3 1.0 copy-done.1
  4.3 0.0 copy-start.2
  4.3 1.0 copy-done.2
  5.2 0.0 copy-start.3
  5.2 0.9 copy-done.3
  6.1 0.0 copy-start.4
  6.1 0.9 copy-done.4
  7.0 0.0 copy-start.5
  7.0 0.7 copy-done.5
  7.7 0.0 copy-start.6
  7.7 0.7 copy-done.6
  8.4 88.7 %shard_map.121 = (f32[56,1024]{1,0:T(8,128)S(1)}, bf16[2,16,16,512]{3,2,1,0:T(8,128)(2,1)S(1)}) custom-call(bf16[56,12288]{1,0:T(8,128)(2,1)S(1)} %copy-done, bf16[56,3072]{1,0:T(8,128)(2,1)S(1)} %copy-done.2, bf16[16,12288]{1,0:T(8,128)(2,1)S(1)} %bitcast.12, bf16[16,3072]{1,0:T(8,128)(2,1)S(1)} %copy-done.4, f32[1,3072]{1,0:T(1,128)S(1)} %bitcast.13, ...), custom_call_target="tpu_custom_call" | custom-call | tf_op jit(solution)/shard_map/pallas_call | solution.py:544
  97.1 0.2 convert_bitcast_fusion
  97.3 0.1 copy.14
  97.4 0.7 slice.9
  98.1 0.9 slice_bitcast_fusion
  99.0 0.7 copy.18
Async XLA Ops:
  1.9 1.3 %copy-start = (bf16[56,12288]{1,0:T(8,128)(2,1)S(1)}, bf16[56,12288]{1,0:T(8,128)(2,1)}, u32[]{:S(2)}) copy-start(bf16[56,12288]{1,0:T(8,128)(2,1)} %inner_h.1) | copy-start | bytes 4128772
  3.3 1.0 copy-start.1
  4.3 1.0 copy-start.2
  5.2 0.9 copy-start.3
  6.1 0.9 copy-start.4
  7.0 0.7 copy-start.5
  7.7 0.7 copy-start.6

commit v2 on v1

--- a/solution.py
+++ b/solution.py
@@ -152,20 +152,24 @@
     barrier = pltpu.get_barrier_semaphore()
     pl.semaphore_signal(barrier, inc=1, device_id=sibling, device_id_type=MESH)
 
-    @pl.loop(1, PLANE)
-    def _(o):
-        pl.semaphore_signal(barrier, inc=1, device_id=plane_device(at_k(o)), device_id_type=MESH)
-
-    @pl.loop(1, Z)
-    def _(o):
-        pl.semaphore_signal(barrier, inc=1, device_id=device(x, y, at_z(o), c), device_id_type=MESH)
+    for neighbour in (above, below):
+        pl.semaphore_signal(barrier, inc=1, device_id=neighbour, device_id_type=MESH)
+    for o in range(1, Y):
+        pl.semaphore_signal(
+            barrier, inc=1, device_id=device(x, at_y(o), z, c), device_id_type=MESH
+        )
+    for o in range(1, X):
+        pl.semaphore_signal(
+            barrier, inc=1, device_id=device(at_x(o), y, z, c), device_id_type=MESH
+        )
 
     for load in loads:
         load.start()
-    pl.semaphore_wait(barrier, 1 + (PLANE - 1) + (Z - 1))
+    pl.semaphore_wait(barrier, 1 + 2 + (Y - 1) + (X - 1))
 
     raw_copy = remote(text_h, raw.at[c], raw_send, raw_recv, sibling)
     raw_copy.start()
+    pending = [raw_copy.wait_send]
     loads[0].wait()
     raw_copy.wait_recv()
 
@@ -203,13 +207,13 @@
         ref = texts.at[c, z, 1, at_y(o)]
         remote(ref, ref, qy_send.at[0], qy_recv.at[at_y(o)], sibling).wait_recv()
 
-    def piece1_up(zz, hop):
-        ref = texts.at[c, zz, 1]
-        return remote(ref, ref, qz_send.at[hop], qz_recv.at[zz], above)
-
-    def piece1_down(zz, hop):
-        ref = texts.at[c, zz, 1]
-        return remote(ref, ref, qz_send.at[UP + hop], qz_recv.at[zz], below)
+    def piece1_up(zz, o, hop):
+        ref = texts.at[c, zz, 1, at_y(o)]
+        return remote(ref, ref, qz_send.at[hop, o], qz_recv.at[zz, at_y(o)], above)
+
+    def piece1_down(zz, o, hop):
+        ref = texts.at[c, zz, 1, at_y(o)]
+        return remote(ref, ref, qz_send.at[UP + hop, o], qz_recv.at[zz, at_y(o)], below)
 
     def across(zz):
         ref = texts.at[c, zz]
@@ -220,13 +224,46 @@
         def _(o):
             piece0_y(zz, o).start()
 
-    @pl.loop(1, Y)
-    def _(o):
-        piece1_y(o).start()
-
     piece0_up(z, 0).start()
     piece0_down(z, 0).start()
+
+    @pl.loop(1, Y)
+    def _(o):
+        piece1_y(o).start()
+
+    piece1_up(z, 0, 0).start()
+    piece1_down(z, 0, 0).start()
     spread0(z)
+
+    def wait_piece0():
+        for hop in range(UP):
+            piece0_up(z, hop).wait_send()
+        for hop in range(DOWN):
+            piece0_down(z, hop).wait_send()
+
+        @pl.loop(1, Y)
+        def _(o):
+            @pl.loop(0, Z)
+            def _(zz):
+                piece0_y(zz, o).wait_send()
+
+    def wait_piece1():
+        @pl.loop(0, Y)
+        def _(o):
+            for hop in range(UP):
+                piece1_up(z, o, hop).wait_send()
+            for hop in range(DOWN):
+                piece1_down(z, o, hop).wait_send()
+
+        @pl.loop(1, Y)
+        def _(o):
+            piece1_y(o).wait_send()
+
+        @pl.loop(0, Z)
+        def _(zz):
+            across(zz).wait_send()
+
+    pending += [wait_piece0, wait_piece1]
 
     def pass0(distance):
         zz = at_z(-distance)
@@ -241,6 +278,19 @@
                 piece0_down(zz, distance).start()
             spread0(zz)
 
+    def pass1(distance, first, last):
+        @pl.loop(first, last)
+        def _(o):
+            zz = at_z(-distance)
+            piece1_up(zz, o, 0).wait_recv()
+            if distance < UP:
+                piece1_up(zz, o, distance).start()
+            if distance <= DOWN:
+                zz = at_z(distance)
+                piece1_down(zz, o, 0).wait_recv()
+                if distance < DOWN:
+                    piece1_down(zz, o, distance).start()
+
     loads[1].wait()
     loads[2].wait()
     step = INNER // 4
@@ -250,13 +300,14 @@
         low = low + nt(inner[:, cols], narrow[:, cols])
     low = low.astype(BF16)
 
+    pass0(1)
+    pass1(1, 0, 1)
+
     @pl.loop(1, Y)
     def _(o):
         piece1_y_wait(o)
-
-    piece1_up(z, 0).start()
-    piece1_down(z, 0).start()
-    pass0(1)
+        piece1_up(z, o, 0).start()
+        piece1_down(z, o, 0).start()
 
     loads[3].wait()
     loads[4].wait()
@@ -269,6 +320,8 @@
     normed[...] = spread
     head_in = (spread * gain[...] + bias[...]).astype(BF16)
     pass0(2)
+    pass1(2, 0, 1)
+    pass1(1, 1, Y)
     loads[7].wait()
     embedding = nn(head_in, head[...])
     inv_len = lax.rsqrt(jnp.sum(embedding * embedding, axis=1, keepdims=True) + norm_eps)
@@ -294,37 +347,32 @@
     def _(o):
         send_images(o).start()
 
+    @pending.append
+    def _():
+        @pl.loop(1, X)
+        def _(o):
+            send_images(o).wait_send()
+
     pass0(3)
+    pass1(3, 0, 1)
+    pass1(2, 1, Y)
+
+    def place(s):
+        odd = lax.rem(s, 2)
+        return at_z((1 - odd) * lax.div(s, 2) - odd * lax.div(s + 1, 2))
+
+    def prepare(s):
+        zz = place(s)
+
+        @pl.loop(1, Y)
+        def _(o):
+            piece0_y_wait(zz, o)
+
+        across(zz).start()
+
+    prepare(jnp.int32(0))
     pass0(4)
-
-    def prepare(s):
-        zz = at_z(lax.rem(s, 2) * -(lax.div(s + 1, 2)) + (1 - lax.rem(s, 2)) * lax.div(s, 2))
-
-        @pl.when(lax.rem(s, 2) == 1)
-        def _():
-            distance = lax.div(s + 1, 2)
-            piece1_up(zz, 0).wait_recv()
-
-            @pl.when(distance < UP)
-            def _():
-                piece1_up(zz, distance).start()
-
-        @pl.when((lax.rem(s, 2) == 0) & (s > 0))
-        def _():
-            distance = lax.div(s, 2)
-            piece1_down(zz, 0).wait_recv()
-
-            @pl.when(distance < DOWN)
-            def _():
-                piece1_down(zz, distance).start()
-
-        @pl.loop(1, Y)
-        def _(o):
-            piece0_y_wait(zz, o)
-
-        across(zz).start()
-
-    prepare(jnp.int32(0))
+    pass1(4, 0, 1)
 
     @pl.loop(1, X)
     def _(o):
@@ -342,11 +390,19 @@
 
     @pl.loop(0, Z)
     def _(s):
+        @pl.when(s == 3)
+        def _():
+            pass1(3, 1, Y)
+
+        @pl.when(s == 6)
+        def _():
+            pass1(4, 1, Y)
+
         @pl.when(s < Z - 1)
         def _():
             prepare(s + 1)
 
-        zz = at_z(lax.rem(s, 2) * -(lax.div(s + 1, 2)) + (1 - lax.rem(s, 2)) * lax.div(s, 2))
+        zz = place(s)
         ref = texts.at[1 - c, zz]
         remote(ref, ref, sib_send.at[0], sib_recv.at[zz], sibling).wait_recv()
         parts = [texts[q // 2, zz, q % 2].reshape(TEXTS, QUARTER) for q in range(4)]
@@ -376,6 +432,12 @@
     for o in range(1, X):
         to_wire(dv_send.at[o - 1], [dv[q, rows_of(at_x(o))] for q in range(4)])
         send_sum(o).start()
+
+    @pending.append
+    def _():
+        @pl.loop(1, X)
+        def _(o):
+            send_sum(o).wait_send()
     total = [dv[q, rows_of(x)] for q in range(4)]
     for o in range(1, X):
         ref = dv_recv.at[at_x(o)]
@@ -385,6 +447,7 @@
     dv_own[...] = derivative
     dv_copy = pltpu.make_async_copy(dv_own, dv_h, out_sem.at[0])
     dv_copy.start()
+    pending.append(dv_copy.wait)
 
     embedding = unit[...]
     along = jnp.sum(embedding * derivative, axis=1, keepdims=True)
@@ -411,6 +474,7 @@
     pair_send[...] = grads[1 - c].astype(BF16)
     pair_copy = remote(pair_send, pair_recv, pair_ssem, pair_rsem, sibling)
     pair_copy.start()
+    pending.append(pair_copy.wait_send)
     pair_copy.wait_recv()
     half[...] = grads[c] + pair_recv[...].astype(F32)
     plane_send[...] = half[...].astype(BF16)
@@ -429,6 +493,12 @@
     def _(o):
         plane_copy(o).start()
 
+    @pending.append
+    def _():
+        @pl.loop(1, PLANE)
+        def _(o):
+            plane_copy(o).wait_send()
+
     plane_recv[k] = plane_send[k]
 
     @pl.loop(1, PLANE)
@@ -446,6 +516,12 @@
     def _(o):
         ring_copy(o).start()
 
+    @pending.append
+    def _():
+        @pl.loop(1, Z)
+        def _(o):
+            ring_copy(o).wait_send()
+
     @pl.loop(1, Z)
     def _(o):
         ref = ring_recv.at[at_z(o)]
@@ -465,7 +541,19 @@
     def _(o):
         back_copy(o).start()
 
+    @pending.append
+    def _():
+        @pl.loop(1, PLANE)
+        def _(o):
+            back_copy(o).wait_send()
+
     last_copy(k).start()
+
+    @pending.append
+    def _():
+        @pl.loop(0, PLANE)
+        def _(kk):
+            last_copy(kk).wait_send()
 
     @pl.loop(1, PLANE)
     def _(o):
@@ -481,49 +569,10 @@
 
     grad_copy = pltpu.make_async_copy(final, grad_h, out_sem.at[1])
     grad_copy.start()
-
-    raw_copy.wait_send()
-    for hop in range(UP):
-        piece0_up(z, hop).wait_send()
-        piece1_up(z, hop).wait_send()
-    for hop in range(DOWN):
-        piece0_down(z, hop).wait_send()
-        piece1_down(z, hop).wait_send()
-
-    @pl.loop(1, Y)
-    def _(o):
-        piece1_y(o).wait_send()
-
-        @pl.loop(0, Z)
-        def _(zz):
-            piece0_y(zz, o).wait_send()
-
-    @pl.loop(0, Z)
-    def _(zz):
-        across(zz).wait_send()
-
-    @pl.loop(1, X)
-    def _(o):
-        send_images(o).wait_send()
-        send_sum(o).wait_send()
-
-    pair_copy.wait_send()
-
-    @pl.loop(1, PLANE)
-    def _(o):
-        plane_copy(o).wait_send()
-        back_copy(o).wait_send()
-
-    @pl.loop(1, Z)
-    def _(o):
-        ring_copy(o).wait_send()
-
-    @pl.loop(0, PLANE)
-    def _(kk):
-        last_copy(kk).wait_send()
-
-    dv_copy.wait()
-    grad_copy.wait()
+    pending.append(grad_copy.wait)
+
+    for wait in pending:
+        wait()
 
 
 def body(
@@ -584,8 +633,8 @@
             dma((Z, Y)),
             dma((Y - 1,)),
             dma((Y,)),
-            dma((UP + DOWN,)),
-            dma((Z,)),
+            dma((UP + DOWN, Y)),
+            dma((Z, Y)),
             dma((Z,)),
             dma((Z,)),
             dma((X - 1,)),
@@ -605,7 +654,7 @@
             dma((2,)),
         ],
         compiler_params=pltpu.CompilerParams(
-            collective_id=0, has_side_effects=True, vmem_limit_bytes=48 * 1024 * 1024
+            collective_id=0, has_side_effects=True, vmem_limit_bytes=64_800_000
         ),
     )(
         gelu_pooled_inner,

time: 100 us -> 86.1 us (0.86)
  Pallas kernels: 88.7 us -> 79.5 us
  local copies, waits for them, and re-layouts: 8.9 us -> 3.34 us
    pallas_call x1, Pallas kernels: 88.7 us -> 79.5 us  [body(): pl.pallas_call(kernel, out_shape=(jax.ShapeDtypeStruct((ROWS, E), F32), j...]
    unnamed x15 -> x1, local copies, waits for them, and re-layouts: 7.2 us -> 1.64 us
    unnamed x1, other arithmetic: 0.16 us -> 1.16 us
where the time goes in v2:
time: 86.1 us; the launch traced here: 85.9 us
  Pallas kernels  79.5 us (92%)
  local copies, waits for them, and re-layouts  3.34 us (4%)
  between operations  1.95 us (2%)
  other arithmetic  1.16 us (1%)
    pallas_call x1, Pallas kernels, body(): pl.pallas_call(kernel, out_shape=(jax.ShapeDtypeStruct((ROWS, E), F32), j...  79.5 us

profile of v2, /device:TPU:1, one launch (start us, length us, event | category | flops | bytes accessed | tf_op | source)
XLA Modules:
  0.0 85.9 jit_solution(9167619315954978500)
XLA Ops:
  1.9 79.5 %shard_map.121 = (f32[56,1024]{1,0:T(8,128)}, bf16[2,16,16,512]{3,2,1,0:T(8,128)(2,1)}) custom-call(bf16[56,12288]{1,0:T(8,128)(2,1)} %inner_h.1, bf16[56,3072]{1,0:T(8,128)(2,1)} %trunk_h.1, bf16[16,12288]{1,0:T(8,128)(2,1)} %bitcast.14, bf16[16,3072]{1,0:T(8,128)(2,1)} %widen_h.1, f32[1,3072]{1,0:T(1,128)} %bitcast.15, f32[1,3072]{1,0:T(1,128)} %bitcast.16, ...), custom_call_target="tpu_custom_call" | custom-call | tf_op jit(solution)/shard_map/pallas_call | solution.py:593
  81.4 1.2 %convert_bitcast_fusion = f32[32,2,8,512]{3,2,1,0:T(8,128)S(1)} fusion(bf16[2,16,16,512]{3,2,1,0:T(8,128)(2,1)} %get-tuple-element.6), kind=kLoop, calls=%fused_computation | loop fusion | flops 262144 | bytes 1572864
  82.6 0.1 copy.14
  82.7 0.7 slice.9
  83.4 0.9 %slice_bitcast_fusion = f32[12288,16]{0,1:T(8,128)} fusion(f32[16,16384]{1,0:T(8,128)S(1)} %bitcast.13), kind=kLoop, calls=%fused_computation.1 | loop fusion | bytes 1572864 | tf_op jit(solution)/shard_map/transpose | solution.py:672
  84.3 1.6 %copy.18 = f32[56,1024]{1,0:T(8,128)} copy(f32[56,1024]{1,0:T(8,128)} %get-tuple-element.10) | data formatting | bytes 458752

commit v3 on v2

v3 whole, which is shorter than its diff:
```python
import jax
import jax.numpy as jnp
from jax import lax
from jax.experimental import pallas as pl
from jax.experimental.pallas import tpu as pltpu
from jax.sharding import PartitionSpec as P

norm_eps = 1e-06
MESH = pl.DeviceIdType.MESH
BF16, F32 = jnp.bfloat16, jnp.float32

X, YL, YH, Z = 4, 2, 2, 8
Y = YL * YH
ROWS = 56
E, DEPTH, INNER, RANK = 1024, 3072, 12288, 16
PC = 640
QC = E - PC
FORE = 384
IMAGES = X * ROWS
SIDE = Y * ROWS
TEXTS = 2 * SIDE
PLANE = X * Y
CUT = 256
WIDE = 2 * CUT
UP, DOWN = Z // 2, Z // 2 - 1


def remote(src, dst, send_sem, recv_sem, device):
    return pltpu.make_async_remote_copy(
        src_ref=src,
        dst_ref=dst,
        send_sem=send_sem,
        recv_sem=recv_sem,
        device_id=device,
        device_id_type=MESH,
    )


def nt(a, b):
    return lax.dot_general(a, b, (((1,), (1,)), ((), ())), preferred_element_type=F32)


def nn(a, b):
    return lax.dot_general(a, b, (((1,), (0,)), ((), ())), preferred_element_type=F32)


def kernel(
    inner_h,
    trunk_h,
    narrow_h,
    widen_h,
    gain_h,
    bias_h,
    head_h,
    text_h,
    sharp_h,
    shift_h,
    dv_h,
    grad_h,
    inner,
    trunk,
    narrow,
    widen,
    gain,
    bias,
    head,
    text,
    sharp_s,
    shift_s,
    tp,
    tq,
    tile,
    image_wire,
    images,
    dv,
    dv_send,
    dv_recv,
    dv_own,
    unit,
    normed,
    grads,
    pair_send,
    pair_recv,
    plane_send,
    plane_recv,
    ring_recv,
    final,
    load_sem,
    pz_send,
    pz_recv,
    py_send,
    py_recv,
    pf_send,
    pf_recv,
    qy_send,
    qy_recv,
    qz_send,
    qz_recv,
    sp_send,
    sp_recv,
    sq_send,
    sq_recv,
    img_send,
    img_recv,
    rs_send,
    rs_recv,
    pair_ssem,
    pair_rsem,
    plane_ssem,
    plane_rsem,
    ring_ssem,
    ring_rsem,
    back_ssem,
    back_rsem,
    last_ssem,
    last_rsem,
    out_sem,
):
    g, d = lax.axis_index("group"), lax.axis_index("dp")
    c, yh = lax.rem(g, 2), lax.div(g, 2)
    z, yl, x = lax.div(d, YL * X), lax.rem(lax.div(d, X), YL), lax.rem(d, X)
    y = yh * YL + yl
    k = y * X + x

    def device(xx, yy, zz, cc):
        return (
            lax.div(yy, YL) * 2 + cc,
            zz * (YL * X) + lax.rem(yy, YL) * X + xx,
        )

    sibling = device(x, y, z, 1 - c)
    above = device(x, y, lax.rem(z + 1, Z), c)
    below = device(x, y, lax.rem(z + Z - 1, Z), c)

    def at_y(o):
        return lax.rem(y + o, Y)

    def at_x(o):
        return lax.rem(x + o, X)

    def at_z(o):
        return lax.rem(z + o + Z, Z)

    def at_k(o):
        return lax.rem(k + o, PLANE)

    def plane_device(kk):
        return device(lax.rem(kk, X), lax.div(kk, X), z, c)

    loads = [
        pltpu.make_async_copy(text_h, text, load_sem.at[0]),
        pltpu.make_async_copy(inner_h, inner, load_sem.at[1]),
        pltpu.make_async_copy(narrow_h, narrow, load_sem.at[2]),
        pltpu.make_async_copy(widen_h, widen, load_sem.at[3]),
        pltpu.make_async_copy(trunk_h, trunk, load_sem.at[4]),
        pltpu.make_async_copy(gain_h, gain, load_sem.at[5]),
        pltpu.make_async_copy(bias_h, bias, load_sem.at[6]),
        pltpu.make_async_copy(head_h, head, load_sem.at[7]),
        pltpu.make_async_copy(sharp_h, sharp_s, load_sem.at[8]),
        pltpu.make_async_copy(shift_h, shift_s, load_sem.at[9]),
    ]
    barrier = pltpu.get_barrier_semaphore()
    pl.semaphore_signal(barrier, inc=1, device_id=sibling, device_id_type=MESH)

    for neighbour in (above, below):
        pl.semaphore_signal(barrier, inc=1, device_id=neighbour, device_id_type=MESH)
    for o in range(1, Y):
        pl.semaphore_signal(
            barrier, inc=1, device_id=device(x, at_y(o), z, c), device_id_type=MESH
        )
    for o in range(1, X):
        pl.semaphore_signal(
            barrier, inc=1, device_id=device(at_x(o), y, z, c), device_id_type=MESH
        )

    for load in loads:
        load.start()
    pl.semaphore_wait(barrier, 1 + 2 + (Y - 1) + (X - 1))

    pending = []

    loads[0].wait()
    rows = text[...].astype(F32)
    rows = rows * lax.rsqrt(jnp.sum(rows * rows, axis=1, keepdims=True) + norm_eps)
    tp[c, z, y] = rows[:, :PC].astype(BF16)
    tq[c, z, y] = rows[:, PC:].astype(BF16)

    def p_up(zz, hop):
        ref = tp.at[c, zz, y]
        return remote(ref, ref, pz_send.at[hop], pz_recv.at[zz], above)

    def p_down(zz, hop):
        ref = tp.at[c, zz, y]
        return remote(ref, ref, pz_send.at[UP + hop], pz_recv.at[zz], below)

    def p_y(zz, i):
        ref = tp.at[c, zz, y]
        to = device(x, at_y((1, Y - 1)[i]), z, c)
        return remote(ref, ref, py_send.at[zz, i], py_recv.at[zz, i], to)

    def p_y_in(zz, i):
        ref = tp.at[c, zz, at_y((Y - 1, 1)[i])]
        return remote(ref, ref, py_send.at[0, 0], py_recv.at[zz, i], sibling)

    def half_of(ref, i):
        return ref.at[:, pl.ds((0, FORE)[i], (FORE, PC - FORE)[i])]

    def p_far(zz, i):
        ref = half_of(tp.at[c, zz, at_y((Y - 1, 1)[i])], i)
        to = device(x, at_y((1, Y - 1)[i]), z, c)
        return remote(ref, ref, pf_send.at[zz, i], pf_recv.at[zz, i], to)

    def p_far_in(zz, i):
        ref = half_of(tp.at[c, zz, at_y(2)], i)
        return remote(ref, ref, pf_send.at[0, 0], pf_recv.at[zz, i], sibling)

    def q_y(o):
        ref = tq.at[c, z, y]
        return remote(ref, ref, qy_send.at[o - 1], qy_recv.at[y], device(x, at_y(o), z, c))

    def q_y_in(o):
        ref = tq.at[c, z, at_y(o)]
        return remote(ref, ref, qy_send.at[0], qy_recv.at[at_y(o)], sibling)

    def q_up(zz, o, hop):
        ref = tq.at[c, zz, at_y(o)]
        return remote(ref, ref, qz_send.at[hop, o], qz_recv.at[zz, at_y(o)], above)

    def q_down(zz, o, hop):
        ref = tq.at[c, zz, at_y(o)]
        return remote(ref, ref, qz_send.at[UP + hop, o], qz_recv.at[zz, at_y(o)], below)

    def p_across(zz):
        ref = tp.at[c, zz]
        return remote(ref, ref, sp_send.at[zz], sp_recv.at[zz], sibling)

    def q_across(zz):
        ref = tq.at[c, zz]
        return remote(ref, ref, sq_send.at[zz], sq_recv.at[zz], sibling)

    def both(distance):
        if distance == 0:
            return [z]
        return [at_z(-distance), at_z(distance)][: 1 + (distance <= DOWN)]

    p_up(z, 0).start()
    p_down(z, 0).start()
    for i in range(2):
        p_y(z, i).start()
    for o in (1, 3, 2):
        q_y(o).start()
    q_up(z, 0, 0).start()
    q_down(z, 0, 0).start()

    @pending.append
    def _():
        for hop in range(UP):
            p_up(z, hop).wait_send()
        for hop in range(DOWN):
            p_down(z, hop).wait_send()

        @pl.loop(0, Z)
        def _(zz):
            for i in range(2):
                p_y(zz, i).wait_send()
                p_far(zz, i).wait_send()
            p_across(zz).wait_send()
            q_across(zz).wait_send()

        for o in range(1, Y):
            q_y(o).wait_send()

        @pl.loop(0, Y)
        def _(o):
            for hop in range(UP):
                q_up(z, o, hop).wait_send()
            for hop in range(DOWN):
                q_down(z, o, hop).wait_send()

    def p_ring(distance):
        zz = at_z(-distance)
        p_up(zz, 0).wait_recv()
        if distance < UP:
            p_up(zz, distance).start()
        if distance <= DOWN:
            zz = at_z(distance)
            p_down(zz, 0).wait_recv()
            if distance < DOWN:
                p_down(zz, distance).start()
        for zz in both(distance):
            for i in range(2):
                p_y(zz, i).start()

    def p_pass(distance):
        for zz in both(distance):
            for i in range(2):
                p_y_in(zz, i).wait_recv()
                p_far(zz, i).start()

    def p_end(distance):
        for zz in both(distance):
            for i in range(2):
                p_far_in(zz, i).wait_recv()
            p_across(zz).start()

    def q_first():
        for o in (1, 3, 2):
            q_y_in(o).wait_recv()
            q_up(z, o, 0).start()
            q_down(z, o, 0).start()

    def q_ring(distance, others):
        for o in others:
            zz = at_z(-distance)
            q_up(zz, o, 0).wait_recv()
            if distance < UP:
                q_up(zz, o, distance).start()
            if distance <= DOWN:
                zz = at_z(distance)
                q_down(zz, o, 0).wait_recv()
                if distance < DOWN:
                    q_down(zz, o, distance).start()

    def q_end(distance):
        for zz in both(distance):
            q_across(zz).start()

    own, rest = (0,), (1, 3, 2)

    loads[1].wait()
    loads[2].wait()
    step = INNER // 4
    low = jnp.zeros((ROWS, RANK), F32)
    for i in range(4):
        cols = pl.ds(i * step, step)
        low = low + nt(inner[:, cols], narrow[:, cols])
    low = low.astype(BF16)

    p_ring(1)
    p_pass(0)
    q_ring(1, own)
    q_first()
    loads[3].wait()
    loads[4].wait()
    loads[5].wait()
    loads[6].wait()
    section = trunk[...].astype(F32) + nn(low, widen[...])
    centred = section - jnp.mean(section, axis=1, keepdims=True)
    inv_std = lax.rsqrt(jnp.mean(centred * centred, axis=1, keepdims=True) + norm_eps)
    spread = centred * inv_std
    normed[...] = spread
    head_in = (spread * gain[...] + bias[...]).astype(BF16)
    p_ring(2)
    p_pass(1)
    q_ring(1, rest)
    q_ring(2, own)
    loads[7].wait()
    embedding = nn(head_in, head[...])
    inv_len = lax.rsqrt(jnp.sum(embedding * embedding, axis=1, keepdims=True) + norm_eps)
    embedding = embedding * inv_len
    unit[...] = embedding

    half = E // 2

    def to_wire(ref, value):
        ref[...] = jnp.concatenate([value[:, :half], value[:, half:]], axis=0).astype(BF16)

    def from_wire(ref):
        value = ref[...].astype(F32)
        return jnp.concatenate([value[:ROWS], value[ROWS:]], axis=1)

    to_wire(image_wire.at[x], embedding)

    def send_images(o):
        ref = image_wire.at[x]
        return remote(ref, ref, img_send.at[o - 1], img_recv.at[x], device(at_x(o), y, z, c))

    @pl.loop(1, X)
    def _(o):
        send_images(o).start()

    @pending.append
    def _():
        @pl.loop(1, X)
        def _(o):
            send_images(o).wait_send()

    p_ring(3)
    p_pass(2)
    q_ring(2, rest)
    q_ring(3, own)
    p_end(0)
    q_end(0)

    @pl.loop(1, X)
    def _(o):
        ref = image_wire.at[at_x(o)]
        remote(ref, ref, img_send.at[0], img_recv.at[at_x(o)], sibling).wait_recv()

    for i in range(0, X, 2):
        two = jnp.concatenate([from_wire(image_wire.at[i]), from_wire(image_wire.at[i + 1])], axis=0)
        images[pl.ds(i * ROWS, 2 * ROWS)] = two.astype(BF16)

    loads[8].wait()
    loads[9].wait()
    sharp = jnp.exp(jnp.full((1, TEXTS), sharp_s[0], F32))
    shift = jnp.full((1, TEXTS), shift_s[0], F32)
    dv[...] = jnp.zeros_like(dv)
    p_ring(4)
    p_pass(3)

    @pl.loop(0, Z)
    def _(s):
        @pl.when(s == 0)
        def _():
            q_ring(3, rest)
            q_ring(4, own)
            p_end(1)
            q_end(1)

        @pl.when(s == 1)
        def _():
            p_pass(4)

        @pl.when(s == 2)
        def _():
            p_end(2)
            q_end(2)

        @pl.when(s == 3)
        def _():
            p_end(3)
            q_end(3)

        @pl.when(s == 5)
        def _():
            q_ring(4, rest)
            p_end(4)
            q_end(4)

        odd = lax.rem(s, 2)
        zz = at_z((1 - odd) * lax.div(s, 2) - odd * lax.div(s + 1, 2))
        for ref, send, recv in ((tp, sp_send, sp_recv), (tq, sq_send, sq_recv)):
            ref = ref.at[1 - c, zz]
            remote(ref, ref, send.at[0], recv.at[zz], sibling).wait_recv()
        for core in range(2):
            part = pl.ds(core * SIDE, SIDE)
            tile[part, :PC] = tp[core, zz].astype(F32).reshape(SIDE, PC).astype(BF16)
            tile[part, PC:] = tq[core, zz].astype(F32).reshape(SIDE, QC).astype(BF16)
        cosine = nt(images[...], tile[...])
        row = lax.broadcasted_iota(jnp.int32, (IMAGES, TEXTS), 0) - x * ROWS
        col = lax.broadcasted_iota(jnp.int32, (IMAGES, TEXTS), 1) - (c * Y + y) * ROWS
        same = (row == col) & (row >= 0) & (row < ROWS) & (s == 0)
        weights = sharp * (jax.nn.sigmoid(sharp * cosine + shift) - jnp.where(same, 1.0, 0.0))
        dv[...] += nn(weights.astype(BF16), tile[...])

    def send_sum(o):
        return remote(
            dv_send.at[o - 1],
            dv_recv.at[x],
            rs_send.at[o - 1],
            rs_recv.at[x],
            device(at_x(o), y, z, c),
        )

    def rows_of(xx):
        return pl.ds(pl.multiple_of(xx * ROWS, 8), ROWS)

    for o in range(1, X):
        to_wire(dv_send.at[o - 1], dv[rows_of(at_x(o))])
        send_sum(o).start()

    @pending.append
    def _():
        @pl.loop(1, X)
        def _(o):
            send_sum(o).wait_send()
    derivative = dv[rows_of(x)]
    for o in range(1, X):
        ref = dv_recv.at[at_x(o)]
        remote(ref, ref, rs_send.at[0], rs_recv.at[at_x(o)], sibling).wait_recv()
        derivative = derivative + from_wire(ref)
    dv_own[...] = derivative
    dv_copy = pltpu.make_async_copy(dv_own, dv_h, out_sem.at[0])
    dv_copy.start()
    pending.append(dv_copy.wait)

    embedding = unit[...]
    along = jnp.sum(embedding * derivative, axis=1, keepdims=True)
    embed_grad = (inv_len * (derivative - embedding * along)).astype(BF16)
    scaled = nt(embed_grad, head[...]) * gain[...]
    spread = normed[...]
    section_grad = inv_std * (
        scaled
        - jnp.mean(scaled, axis=1, keepdims=True)
        - spread * jnp.mean(scaled * spread, axis=1, keepdims=True)
    )
    section_grad = section_grad.astype(BF16)
    back = nt(widen[...], section_grad).astype(BF16)
    up = lax.dot_general(low, section_grad, (((0,), (0,)), ((), ())), preferred_element_type=F32)
    n_down, n_up = INNER // WIDE, DEPTH // WIDE
    for i in range(2 * PLANE):
        if i < n_down:
            value = nn(back, inner[:, pl.ds(i * WIDE, WIDE)])
        elif i < n_down + n_up:
            value = up[:, (i - n_down) * WIDE : (i - n_down + 1) * WIDE]
        else:
            value = jnp.zeros((RANK, WIDE), F32)
        for h in range(2):
            grads[h, i // PLANE, i % PLANE] = value[:, h * CUT : (h + 1) * CUT]

    def pair_copy(h):
        return remote(pair_send.at[h], pair_recv.at[h], pair_ssem.at[h], pair_rsem.at[h], sibling)

    def plane_copy(h, o):
        kk = at_k(o)
        return remote(
            plane_send.at[h, kk],
            plane_recv.at[h, k],
            plane_ssem.at[h, o - 1],
            plane_rsem.at[h, k],
            plane_device(kk),
        )

    def plane_in(h, o):
        ref = plane_recv.at[h, at_k(o)]
        return remote(ref, ref, plane_ssem.at[0, 0], plane_rsem.at[h, at_k(o)], sibling)

    def ring_copy(h, o):
        ref = ring_recv.at[h, z]
        to = device(x, y, at_z(o), c)
        return remote(ref, ref, ring_ssem.at[h, o - 1], ring_rsem.at[h, z], to)

    def ring_in(h, o):
        ref = ring_recv.at[h, at_z(o)]
        return remote(ref, ref, ring_ssem.at[0, 0], ring_rsem.at[h, at_z(o)], sibling)

    def back_copy(h, o):
        ref = final.at[h, c, k]
        return remote(ref, ref, back_ssem.at[h, o - 1], back_rsem.at[h, k], plane_device(at_k(o)))

    def back_in(h, o):
        ref = final.at[h, c, at_k(o)]
        return remote(ref, ref, back_ssem.at[0, 0], back_rsem.at[h, at_k(o)], sibling)

    def last_copy(h, kk):
        ref = final.at[h, c, kk]
        return remote(ref, ref, last_ssem.at[h, kk], last_rsem.at[h, kk], sibling)

    def last_in(h, kk):
        ref = final.at[h, 1 - c, kk]
        return remote(ref, ref, last_ssem.at[0, 0], last_rsem.at[h, kk], sibling)

    def out_copy(h, core):
        return pltpu.make_async_copy(
            final.at[h, core], grad_h.at[h, core], out_sem.at[1 + 2 * h + core]
        )

    for h in range(2):
        pair_send[h] = grads[h, 1 - c].astype(BF16)
        pair_copy(h).start()
    for h in range(2):
        pair_copy(h).wait_recv()
        plane_send[h] = (grads[h, c] + pair_recv[h].astype(F32)).astype(BF16)

        @pl.loop(1, PLANE)
        def _(o):
            plane_copy(h, o).start()

        plane_recv[h, k] = plane_send[h, k]
    for h in range(2):

        @pl.loop(1, PLANE)
        def _(o):
            plane_in(h, o).wait_recv()

        ring_recv[h, z] = jnp.sum(plane_recv[h].astype(F32), axis=0).astype(BF16)

        @pl.loop(1, Z)
        def _(o):
            ring_copy(h, o).start()

    for h in range(2):

        @pl.loop(1, Z)
        def _(o):
            ring_in(h, o).wait_recv()

        final[h, c, k] = jnp.sum(ring_recv[h].astype(F32), axis=0).astype(BF16)

        @pl.loop(1, PLANE)
        def _(o):
            back_copy(h, o).start()

        last_copy(h, k).start()
    for h in range(2):

        @pl.loop(1, PLANE)
        def _(o):
            back_in(h, o).wait_recv()
            last_copy(h, at_k(o)).start()

        out_copy(h, c).start()
    for h in range(2):

        @pl.loop(0, PLANE)
        def _(kk):
            last_in(h, kk).wait_recv()

        out_copy(h, 1 - c).start()

    @pending.append
    def _():
        for h in range(2):
            pair_copy(h).wait_send()

            @pl.loop(1, PLANE)
            def _(o):
                plane_copy(h, o).wait_send()
                back_copy(h, o).wait_send()

            @pl.loop(1, Z)
            def _(o):
                ring_copy(h, o).wait_send()

            @pl.loop(0, PLANE)
            def _(kk):
                last_copy(h, kk).wait_send()

            for core in range(2):
                out_copy(h, core).wait()

    for wait in pending:
        wait()


def finish(
    dv_h, grad_h, dv_out, down_out, up_out, dv, pieces, whole, in_sem, dv_sem, down_sem, up_sem
):
    reads = [
        pltpu.make_async_copy(dv_h, dv, in_sem.at[0]),
        pltpu.make_async_copy(grad_h, pieces, in_sem.at[1]),
    ]
    for read in reads:
        read.start()
    for read in reads:
        read.wait()
    dv_copy = pltpu.make_async_copy(dv, dv_out, dv_sem)
    dv_copy.start()

    def out(i):
        if i < INNER // DEPTH:
            cols = pl.ds(i * DEPTH, DEPTH)
            return pltpu.make_async_copy(whole.at[:, cols], down_out.at[:, cols], down_sem.at[i])
        return pltpu.make_async_copy(whole.at[:, pl.ds(INNER, DEPTH)], up_out, up_sem)

    count = (INNER + DEPTH) // DEPTH
    for i in range(count):
        for j in range(i * DEPTH // CUT, (i + 1) * DEPTH // CUT):
            piece = pieces[j % 2, j // 2 // PLANE, j // 2 % PLANE]
            whole[:, pl.ds(j * CUT, CUT)] = piece.astype(F32)
        out(i).start()
    for i in range(count):
        out(i).wait()
    dv_copy.wait()


def body(
    gelu_pooled_inner,
    frozen_pooled_trunk_result,
    narrowing_weight,
    widening_weight,
    closing_standardize_multiplier,
    closing_standardize_addend,
    closing_projection_weight,
    sentence_encodings,
    logged_sharpening,
    sigmoid_threshold_term,
):
    anywhere = pl.BlockSpec(memory_space=pl.ANY)
    dma = pltpu.SemaphoreType.DMA
    derivative, pieces = pl.pallas_call(
        kernel,
        out_shape=(
            jax.ShapeDtypeStruct((ROWS, E), F32),
            jax.ShapeDtypeStruct((2, 2, PLANE, RANK, CUT), BF16),
        ),
        in_specs=[anywhere] * 8 + [pl.BlockSpec(memory_space=pltpu.HBM)] * 2,
        out_specs=(anywhere, anywhere),
        scratch_shapes=[
            pltpu.VMEM((ROWS, INNER), BF16),
            pltpu.VMEM((ROWS, DEPTH), BF16),
            pltpu.VMEM((RANK, INNER), BF16),
            pltpu.VMEM((RANK, DEPTH), BF16),
            pltpu.VMEM((1, DEPTH), F32),
            pltpu.VMEM((1, DEPTH), F32),
            pltpu.VMEM((DEPTH, E), BF16),
            pltpu.VMEM((ROWS, E), BF16),
            pltpu.SMEM((1,), F32),
            pltpu.SMEM((1,), F32),
            pltpu.VMEM((2, Z, Y, ROWS, PC), BF16),
            pltpu.VMEM((2, Z, Y, ROWS, QC), BF16),
            pltpu.VMEM((TEXTS, E), BF16),
            pltpu.VMEM((X, 2 * ROWS, E // 2), BF16),
            pltpu.VMEM((IMAGES, E), BF16),
            pltpu.VMEM((IMAGES, E), F32),
            pltpu.VMEM((X - 1, 2 * ROWS, E // 2), BF16),
            pltpu.VMEM((X, 2 * ROWS, E // 2), BF16),
            pltpu.VMEM((ROWS, E), F32),
            pltpu.VMEM((ROWS, E), F32),
            pltpu.VMEM((ROWS, DEPTH), F32),
            pltpu.VMEM((2, 2, PLANE, RANK, CUT), F32),
            pltpu.VMEM((2, PLANE, RANK, CUT), BF16),
            pltpu.VMEM((2, PLANE, RANK, CUT), BF16),
            pltpu.VMEM((2, PLANE, RANK, CUT), BF16),
            pltpu.VMEM((2, PLANE, RANK, CUT), BF16),
            pltpu.VMEM((2, Z, RANK, CUT), BF16),
            pltpu.VMEM((2, 2, PLANE, RANK, CUT), BF16),
            dma((10,)),
            dma((UP + DOWN,)),
            dma((Z,)),
            dma((Z, 2)),
            dma((Z, 2)),
            dma((Z, 2)),
            dma((Z, 2)),
            dma((Y - 1,)),
            dma((Y,)),
            dma((UP + DOWN, Y)),
            dma((Z, Y)),
            dma((Z,)),
            dma((Z,)),
            dma((Z,)),
            dma((Z,)),
            dma((X - 1,)),
            dma((X,)),
            dma((X - 1,)),
            dma((X,)),
            dma((2,)),
            dma((2,)),
            dma((2, PLANE - 1)),
            dma((2, PLANE)),
            dma((2, Z - 1)),
            dma((2, Z)),
            dma((2, PLANE - 1)),
            dma((2, PLANE)),
            dma((2, PLANE)),
            dma((2, PLANE)),
            dma((5,)),
        ],
        compiler_params=pltpu.CompilerParams(
            collective_id=0, has_side_effects=True, vmem_limit_bytes=64_800_000
        ),
    )(
        gelu_pooled_inner,
        frozen_pooled_trunk_result,
        narrowing_weight.T,
        widening_weight,
        closing_standardize_multiplier.reshape(1, DEPTH),
        closing_standardize_addend.reshape(1, DEPTH),
        closing_projection_weight,
        sentence_encodings,
        logged_sharpening,
        sigmoid_threshold_term,
    )
    derivative, down, up = pl.pallas_call(
        finish,
        out_shape=(
            jax.ShapeDtypeStruct((ROWS, E), F32),
            jax.ShapeDtypeStruct((RANK, INNER), F32),
            jax.ShapeDtypeStruct((RANK, DEPTH), F32),
        ),
        in_specs=[anywhere] * 2,
        out_specs=(anywhere,) * 3,
        scratch_shapes=[
            pltpu.VMEM((ROWS, E), F32),
            pltpu.VMEM((2, 2, PLANE, RANK, CUT), BF16),
            pltpu.VMEM((RANK, INNER + DEPTH), F32),
            dma((2,)),
            dma,
            dma((INNER // DEPTH,)),
            dma,
        ],
        compiler_params=pltpu.CompilerParams(vmem_limit_bytes=64_800_000),
    )(derivative, pieces)
    return derivative, down.T, up


def solution(mesh):
    rows = P(("group", "dp"), None)
    return jax.shard_map(
        body,
        mesh=mesh,
        in_specs=(rows, rows, P(), P(), P(), P(), P(), rows, P(), P()),
        out_specs=(rows, P(), P()),
        check_vma=False,
    )
```

time: 86.1 us -> 79.4 us (0.922)
  local copies, waits for them, and re-layouts: 3.34 us -> 0 us
  Pallas kernels: 79.5 us -> 77.4 us
  other arithmetic: 1.16 us -> 0 us
    pallas_call x1, Pallas kernels: 79.5 us -> 75.1 us  [body(): pl.pallas_call(kernel, out_shape=(jax.ShapeDtypeStruct((ROWS, E), F32), j...]
    pallas_call x0 -> x1, Pallas kernels: none -> 2.25 us  [body(): pl.pallas_call(finish, out_shape=(jax.ShapeDtypeStruct((ROWS, E), F32), j...]
    unnamed x1 -> x0, local copies, waits for them, and re-layouts: 1.64 us -> none
    unnamed x1 -> x0, other arithmetic: 1.16 us -> none
    transpose x1 -> x0, local copies, waits for them, and re-layouts: 0.93 us -> none  [body(): return (derivative, pieces[:, :INNER].T, pieces[:, INNER:INNER + DEPTH])]
where the time goes in v3:
time: 79.4 us; the launch traced here: 79.3 us
  Pallas kernels  77.4 us (97%)
  between operations  1.93 us (2%)
    pallas_call x1, Pallas kernels, body(): pl.pallas_call(kernel, out_shape=(jax.ShapeDtypeStruct((ROWS, E), F32), j...  75.1 us
    pallas_call x1, Pallas kernels, body(): pl.pallas_call(finish, out_shape=(jax.ShapeDtypeStruct((ROWS, E), F32), j...  2.25 us

profile of v3, /device:TPU:1, one launch (start us, length us, event | category | flops | bytes accessed | tf_op | source)
XLA Modules:
  0.0 79.3 jit_solution(14290179176664215035)
XLA Ops:
  1.9 75.1 %shard_map.121 = (f32[56,1024]{1,0:T(8,128)}, bf16[2,2,16,16,256]{4,3,2,1,0:T(8,128)(2,1)}) custom-call(bf16[56,12288]{1,0:T(8,128)(2,1)} %inner_h.1, bf16[56,3072]{1,0:T(8,128)(2,1)} %trunk_h.1, bf16[16,12288]{1,0:T(8,128)(2,1)} %bitcast.4, bf16[16,3072]{1,0:T(8,128)(2,1)} %widen_h.1, f32[1,3072]{1,0:T(1,128)} %bitcast.5, f32[1,3072]{1,0:T(1,128)} %bitcast.6, ...), custom_call_target="tpu_custom_call" | custom-call | tf_op jit(solution)/shard_map/pallas_call | solution.py:682
  77.1 2.2 %shard_map.122 = (f32[56,1024]{1,0:T(8,128)}, f32[16,12288]{1,0:T(8,128)}, f32[16,3072]{1,0:T(8,128)}) custom-call(f32[56,1024]{1,0:T(8,128)} %get-tuple-element.8.dv_h, bf16[2,2,16,16,256]{4,3,2,1,0:T(8,128)(2,1)} %get-tuple-element.9.grad_h), custom_call_target="tpu_custom_call" | custom-call | tf_op jit(solution)/shard_map/pallas_call | solution.py:765

commit v4 on v3

--- a/solution.py
+++ b/solution.py
@@ -15,14 +15,14 @@
 E, DEPTH, INNER, RANK = 1024, 3072, 12288, 16
 PC = 640
 QC = E - PC
-FORE = 384
-IMAGES = X * ROWS
-SIDE = Y * ROWS
-TEXTS = 2 * SIDE
+FORE = 256
+SIDE = X * ROWS
+IMAGES = 2 * SIDE
+TEXTS = Y * ROWS
 PLANE = X * Y
 CUT = 256
 WIDE = 2 * CUT
-UP, DOWN = Z // 2, Z // 2 - 1
+HOPS = Z // 2 - 1
 
 
 def remote(src, dst, send_sem, recv_sem, device):
@@ -73,11 +73,14 @@
     image_wire,
     images,
     dv,
+    cross_send,
+    cross_recv,
     dv_send,
     dv_recv,
     dv_own,
     unit,
     normed,
+    section,
     grads,
     pair_send,
     pair_recv,
@@ -88,6 +91,8 @@
     load_sem,
     pz_send,
     pz_recv,
+    pt_send,
+    pt_recv,
     py_send,
     py_recv,
     pf_send,
@@ -96,12 +101,12 @@
     qy_recv,
     qz_send,
     qz_recv,
-    sp_send,
-    sp_recv,
-    sq_send,
-    sq_recv,
     img_send,
     img_recv,
+    over_send,
+    over_recv,
+    cross_ssem,
+    cross_rsem,
     rs_send,
     rs_recv,
     pair_ssem,
@@ -159,6 +164,7 @@
         pltpu.make_async_copy(sharp_h, sharp_s, load_sem.at[8]),
         pltpu.make_async_copy(shift_h, shift_s, load_sem.at[9]),
     ]
+    loads[0].start()
     barrier = pltpu.get_barrier_semaphore()
     pl.semaphore_signal(barrier, inc=1, device_id=sibling, device_id_type=MESH)
 
@@ -173,10 +179,8 @@
             barrier, inc=1, device_id=device(at_x(o), y, z, c), device_id_type=MESH
         )
 
-    for load in loads:
+    for load in loads[1:]:
         load.start()
-    pl.semaphore_wait(barrier, 1 + 2 + (Y - 1) + (X - 1))
-
     pending = []
 
     loads[0].wait()
@@ -185,25 +189,31 @@
     tp[c, z, y] = rows[:, :PC].astype(BF16)
     tq[c, z, y] = rows[:, PC:].astype(BF16)
 
+    pl.semaphore_wait(barrier, 1 + 2 + (Y - 1) + (X - 1))
+
     def p_up(zz, hop):
         ref = tp.at[c, zz, y]
         return remote(ref, ref, pz_send.at[hop], pz_recv.at[zz], above)
 
     def p_down(zz, hop):
         ref = tp.at[c, zz, y]
-        return remote(ref, ref, pz_send.at[UP + hop], pz_recv.at[zz], below)
+        return remote(ref, ref, pz_send.at[HOPS + hop], pz_recv.at[zz], below)
+
+    def half_of(ref, i):
+        return ref.at[:, pl.ds((0, FORE)[i], (FORE, PC - FORE)[i])]
+
+    def p_turn(zz, i):
+        ref = half_of(tp.at[c, zz, y], i)
+        return remote(ref, ref, pt_send.at[i], pt_recv.at[i], (above, below)[i])
 
     def p_y(zz, i):
         ref = tp.at[c, zz, y]
-        to = device(x, at_y((1, Y - 1)[i]), z, c)
+        to = device(x, at_y((1, Y - 1, 2)[i]), z, c)
         return remote(ref, ref, py_send.at[zz, i], py_recv.at[zz, i], to)
 
     def p_y_in(zz, i):
-        ref = tp.at[c, zz, at_y((Y - 1, 1)[i])]
+        ref = tp.at[c, zz, at_y((Y - 1, 1, 2)[i])]
         return remote(ref, ref, py_send.at[0, 0], py_recv.at[zz, i], sibling)
-
-    def half_of(ref, i):
-        return ref.at[:, pl.ds((0, FORE)[i], (FORE, PC - FORE)[i])]
 
     def p_far(zz, i):
         ref = half_of(tp.at[c, zz, at_y((Y - 1, 1)[i])], i)
@@ -228,80 +238,84 @@
 
     def q_down(zz, o, hop):
         ref = tq.at[c, zz, at_y(o)]
-        return remote(ref, ref, qz_send.at[UP + hop, o], qz_recv.at[zz, at_y(o)], below)
-
-    def p_across(zz):
-        ref = tp.at[c, zz]
-        return remote(ref, ref, sp_send.at[zz], sp_recv.at[zz], sibling)
-
-    def q_across(zz):
-        ref = tq.at[c, zz]
-        return remote(ref, ref, sq_send.at[zz], sq_recv.at[zz], sibling)
+        return remote(ref, ref, qz_send.at[HOPS + 1 + hop, o], qz_recv.at[zz, at_y(o)], below)
 
     def both(distance):
-        if distance == 0:
-            return [z]
-        return [at_z(-distance), at_z(distance)][: 1 + (distance <= DOWN)]
+        if distance in (0, Z // 2):
+            return [at_z(distance)]
+        return [at_z(-distance), at_z(distance)]
+
+    def p_spread(zz, whole):
+        for i in range(2 + whole):
+            p_y(zz, i).start()
 
     p_up(z, 0).start()
     p_down(z, 0).start()
-    for i in range(2):
-        p_y(z, i).start()
+    p_spread(z, False)
     for o in (1, 3, 2):
         q_y(o).start()
     q_up(z, 0, 0).start()
     q_down(z, 0, 0).start()
 
+    def last_hop(o):
+        return (q_up, q_down)[o % 2]
+
     @pending.append
     def _():
-        for hop in range(UP):
+        for hop in range(HOPS):
             p_up(z, hop).wait_send()
-        for hop in range(DOWN):
             p_down(z, hop).wait_send()
+        for i in range(2):
+            p_turn(z, i).wait_send()
 
         @pl.loop(0, Z)
         def _(zz):
             for i in range(2):
                 p_y(zz, i).wait_send()
-                p_far(zz, i).wait_send()
-            p_across(zz).wait_send()
-            q_across(zz).wait_send()
-
+
+        @pl.loop(0, Z - 1)
+        def _(zz):
+            for i in range(2):
+                p_far(at_z(zz + Z // 2 + 1), i).wait_send()
+
+        p_y(at_z(Z // 2), 2).wait_send()
         for o in range(1, Y):
             q_y(o).wait_send()
-
-        @pl.loop(0, Y)
-        def _(o):
-            for hop in range(UP):
+        for o in range(Y):
+            for hop in range(HOPS):
                 q_up(z, o, hop).wait_send()
-            for hop in range(DOWN):
                 q_down(z, o, hop).wait_send()
+            last_hop(o)(z, o, HOPS).wait_send()
 
     def p_ring(distance):
-        zz = at_z(-distance)
-        p_up(zz, 0).wait_recv()
-        if distance < UP:
-            p_up(zz, distance).start()
-        if distance <= DOWN:
+        if distance > HOPS:
             zz = at_z(distance)
-            p_down(zz, 0).wait_recv()
-            if distance < DOWN:
-                p_down(zz, distance).start()
-        for zz in both(distance):
             for i in range(2):
-                p_y(zz, i).start()
+                p_turn(zz, i).wait_recv()
+            p_spread(zz, True)
+            return
+        for i, (send, zz) in enumerate(((p_up, at_z(-distance)), (p_down, at_z(distance)))):
+            send(zz, 0).wait_recv()
+            if distance < HOPS:
+                send(zz, distance).start()
+            else:
+                p_turn(zz, i).start()
+            p_spread(zz, False)
 
     def p_pass(distance):
         for zz in both(distance):
             for i in range(2):
                 p_y_in(zz, i).wait_recv()
-                p_far(zz, i).start()
+                if distance <= HOPS:
+                    p_far(zz, i).start()
 
     def p_end(distance):
         for zz in both(distance):
-            for i in range(2):
-                p_far_in(zz, i).wait_recv()
-            p_across(zz).start()
+            if distance <= HOPS:
+                for i in range(2):
+                    p_far_in(zz, i).wait_recv()
+            else:
+                p_y_in(zz, 2).wait_recv()
 
     def q_first():
         for o in (1, 3, 2):
@@ -311,19 +325,11 @@
 
     def q_ring(distance, others):
         for o in others:
-            zz = at_z(-distance)
-            q_up(zz, o, 0).wait_recv()
-            if distance < UP:
-                q_up(zz, o, distance).start()
-            if distance <= DOWN:
-                zz = at_z(distance)
-                q_down(zz, o, 0).wait_recv()
-                if distance < DOWN:
-                    q_down(zz, o, distance).start()
-
-    def q_end(distance):
-        for zz in both(distance):
-            q_across(zz).start()
+            for send, zz in ((q_up, at_z(-distance)), (q_down, at_z(distance))):
+                if distance <= HOPS or send is last_hop(o):
+                    send(zz, o, 0).wait_recv()
+                if distance < HOPS or (distance == HOPS and send is last_hop(o)):
+                    send(zz, o, distance).start()
 
     own, rest = (0,), (1, 3, 2)
 
@@ -336,24 +342,20 @@
         low = low + nt(inner[:, cols], narrow[:, cols])
     low = low.astype(BF16)
 
+    loads[3].wait()
+    loads[4].wait()
+    loads[5].wait()
+    loads[6].wait()
+    trailing = trunk[...].astype(F32) + nn(low, widen[...])
+    centred = trailing - jnp.mean(trailing, axis=1, keepdims=True)
+    inv_std = lax.rsqrt(jnp.mean(centred * centred, axis=1, keepdims=True) + norm_eps)
+    spread = centred * inv_std
+    normed[...] = spread
+    head_in = (spread * gain[...] + bias[...]).astype(BF16)
     p_ring(1)
     p_pass(0)
     q_ring(1, own)
     q_first()
-    loads[3].wait()
-    loads[4].wait()
-    loads[5].wait()
-    loads[6].wait()
-    section = trunk[...].astype(F32) + nn(low, widen[...])
-    centred = section - jnp.mean(section, axis=1, keepdims=True)
-    inv_std = lax.rsqrt(jnp.mean(centred * centred, axis=1, keepdims=True) + norm_eps)
-    spread = centred * inv_std
-    normed[...] = spread
-    head_in = (spread * gain[...] + bias[...]).astype(BF16)
-    p_ring(2)
-    p_pass(1)
-    q_ring(1, rest)
-    q_ring(2, own)
     loads[7].wait()
     embedding = nn(head_in, head[...])
     inv_len = lax.rsqrt(jnp.sum(embedding * embedding, axis=1, keepdims=True) + norm_eps)
@@ -369,15 +371,21 @@
         value = ref[...].astype(F32)
         return jnp.concatenate([value[:ROWS], value[ROWS:]], axis=1)
 
-    to_wire(image_wire.at[x], embedding)
+    to_wire(image_wire.at[c, x], embedding)
 
     def send_images(o):
-        ref = image_wire.at[x]
+        ref = image_wire.at[c, x]
         return remote(ref, ref, img_send.at[o - 1], img_recv.at[x], device(at_x(o), y, z, c))
+
+    def images_over(xx):
+        ref = image_wire.at[c, xx]
+        return remote(ref, ref, over_send.at[xx], over_recv.at[xx], sibling)
 
     @pl.loop(1, X)
     def _(o):
         send_images(o).start()
+
+    images_over(x).start()
 
     @pending.append
     def _():
@@ -385,71 +393,83 @@
         def _(o):
             send_images(o).wait_send()
 
+        @pl.loop(0, X)
+        def _(xx):
+            images_over(xx).wait_send()
+
+    p_ring(2)
+    p_pass(1)
+    q_ring(1, rest)
+    q_ring(2, own)
     p_ring(3)
     p_pass(2)
     q_ring(2, rest)
     q_ring(3, own)
     p_end(0)
-    q_end(0)
 
     @pl.loop(1, X)
     def _(o):
-        ref = image_wire.at[at_x(o)]
+        ref = image_wire.at[c, at_x(o)]
         remote(ref, ref, img_send.at[0], img_recv.at[at_x(o)], sibling).wait_recv()
-
-    for i in range(0, X, 2):
-        two = jnp.concatenate([from_wire(image_wire.at[i]), from_wire(image_wire.at[i + 1])], axis=0)
-        images[pl.ds(i * ROWS, 2 * ROWS)] = two.astype(BF16)
+        images_over(at_x(o)).start()
+
+    @pl.loop(0, X)
+    def _(xx):
+        ref = image_wire.at[1 - c, xx]
+        remote(ref, ref, over_send.at[0], over_recv.at[xx], sibling).wait_recv()
+
+    for i in range(0, 2 * X, 2):
+        two = [from_wire(image_wire.at[j // X, j % X]) for j in (i, i + 1)]
+        images[pl.ds(i * ROWS, 2 * ROWS)] = jnp.concatenate(two, axis=0).astype(BF16)
 
     loads[8].wait()
     loads[9].wait()
-    sharp = jnp.exp(jnp.full((1, TEXTS), sharp_s[0], F32))
-    shift = jnp.full((1, TEXTS), shift_s[0], F32)
+    sharp = jnp.exp(jnp.full((1, 2 * TEXTS), sharp_s[0], F32))
+    shift = jnp.full((1, 2 * TEXTS), shift_s[0], F32)
     dv[...] = jnp.zeros_like(dv)
-    p_ring(4)
-    p_pass(3)
-
-    @pl.loop(0, Z)
+
+    @pl.loop(0, Z // 2 + 1)
     def _(s):
-        @pl.when(s == 0)
+        @pl.when(s == 1)
+        def _():
+            p_ring(4)
+            p_pass(3)
+            p_end(1)
+
+        @pl.when(s == 2)
         def _():
             q_ring(3, rest)
-            q_ring(4, own)
-            p_end(1)
-            q_end(1)
-
-        @pl.when(s == 1)
-        def _():
-            p_pass(4)
-
-        @pl.when(s == 2)
-        def _():
             p_end(2)
-            q_end(2)
 
         @pl.when(s == 3)
         def _():
             p_end(3)
-            q_end(3)
-
-        @pl.when(s == 5)
+
+        @pl.when(s == 4)
         def _():
-            q_ring(4, rest)
+            q_ring(4, own + rest)
+            p_pass(4)
             p_end(4)
-            q_end(4)
-
-        odd = lax.rem(s, 2)
-        zz = at_z((1 - odd) * lax.div(s, 2) - odd * lax.div(s + 1, 2))
-        for ref, send, recv in ((tp, sp_send, sp_recv), (tq, sq_send, sq_recv)):
-            ref = ref.at[1 - c, zz]
-            remote(ref, ref, send.at[0], recv.at[zz], sibling).wait_recv()
-        for core in range(2):
-            part = pl.ds(core * SIDE, SIDE)
-            tile[part, :PC] = tp[core, zz].astype(F32).reshape(SIDE, PC).astype(BF16)
-            tile[part, PC:] = tq[core, zz].astype(F32).reshape(SIDE, QC).astype(BF16)
+
+        def fill(i, zz):
+            part = pl.ds(i * TEXTS, TEXTS)
+            tile[part, :PC] = tp[c, zz].astype(F32).reshape(TEXTS, PC).astype(BF16)
+            tile[part, PC:] = tq[c, zz].astype(F32).reshape(TEXTS, QC).astype(BF16)
+
+        fill(0, at_z(-s))
+        single = (s == 0) | (s == Z // 2)
+
+        @pl.when(single)
+        def _():
+            tile[pl.ds(TEXTS, TEXTS)] = jnp.zeros((TEXTS, E), BF16)
+
+        @pl.when(jnp.logical_not(single))
+        def _():
+            fill(1, at_z(s))
+
         cosine = nt(images[...], tile[...])
-        row = lax.broadcasted_iota(jnp.int32, (IMAGES, TEXTS), 0) - x * ROWS
-        col = lax.broadcasted_iota(jnp.int32, (IMAGES, TEXTS), 1) - (c * Y + y) * ROWS
+        row = lax.broadcasted_iota(jnp.int32, cosine.shape, 0) - (c * X + x) * ROWS
+        col = lax.broadcasted_iota(jnp.int32, cosine.shape, 1) - y * ROWS
         same = (row == col) & (row >= 0) & (row < ROWS) & (s == 0)
         weights = sharp * (jax.nn.sigmoid(sharp * cosine + shift) - jnp.where(same, 1.0, 0.0))
         dv[...] += nn(weights.astype(BF16), tile[...])
@@ -463,19 +483,32 @@
             device(at_x(o), y, z, c),
         )
 
-    def rows_of(xx):
-        return pl.ds(pl.multiple_of(xx * ROWS, 8), ROWS)
-
-    for o in range(1, X):
-        to_wire(dv_send.at[o - 1], dv[rows_of(at_x(o))])
-        send_sum(o).start()
+    def cross(o):
+        return remote(
+            cross_send.at[o], cross_recv.at[o], cross_ssem.at[o], cross_rsem.at[o], sibling
+        )
+
+    def rows_of(core, xx):
+        return pl.ds(pl.multiple_of((core * X + xx) * ROWS, 8), ROWS)
+
+    order = (*range(1, X), 0)
+    for o in order:
+        to_wire(cross_send.at[o], dv[rows_of(1 - c, at_x(o))])
+        cross(o).start()
+    for o in order:
+        cross(o).wait_recv()
+        derivative = dv[rows_of(c, at_x(o))] + from_wire(cross_recv.at[o])
+        if o > 0:
+            to_wire(dv_send.at[o - 1], derivative)
+            send_sum(o).start()
 
     @pending.append
     def _():
-        @pl.loop(1, X)
-        def _(o):
-            send_sum(o).wait_send()
-    derivative = dv[rows_of(x)]
+        for o in range(X):
+            cross(o).wait_send()
+            if o > 0:
+                send_sum(o).wait_send()
+
     for o in range(1, X):
         ref = dv_recv.at[at_x(o)]
         remote(ref, ref, rs_send.at[0], rs_recv.at[at_x(o)], sibling).wait_recv()
@@ -496,18 +529,20 @@
         - spread * jnp.mean(scaled * spread, axis=1, keepdims=True)
     )
     section_grad = section_grad.astype(BF16)
+    section[...] = section_grad
     back = nt(widen[...], section_grad).astype(BF16)
-    up = lax.dot_general(low, section_grad, (((0,), (0,)), ((), ())), preferred_element_type=F32)
-    n_down, n_up = INNER // WIDE, DEPTH // WIDE
-    for i in range(2 * PLANE):
+
+    n_down, n_up = INNER // WIDE // 2, DEPTH // WIDE // 2
+
+    def piece(i, core):
         if i < n_down:
-            value = nn(back, inner[:, pl.ds(i * WIDE, WIDE)])
-        elif i < n_down + n_up:
-            value = up[:, (i - n_down) * WIDE : (i - n_down + 1) * WIDE]
-        else:
-            value = jnp.zeros((RANK, WIDE), F32)
-        for h in range(2):
-            grads[h, i // PLANE, i % PLANE] = value[:, h * CUT : (h + 1) * CUT]
+            cols = pl.ds(pl.multiple_of((2 * i + core) * WIDE, WIDE), WIDE)
+            return nn(back, inner[:, cols])
+        if i < n_down + n_up:
+            cols = pl.ds(pl.multiple_of((2 * (i - n_down) + core) * WIDE, WIDE), WIDE)
+            dims = (((0,), (0,)), ((), ()))
+            return lax.dot_general(low, section[:, cols], dims, preferred_element_type=F32)
+        return jnp.zeros((RANK, WIDE), F32)
 
     def pair_copy(h):
         return remote(pair_send.at[h], pair_recv.at[h], pair_ssem.at[h], pair_rsem.at[h], sibling)
@@ -556,12 +591,19 @@
             final.at[h, core], grad_h.at[h, core], out_sem.at[1 + 2 * h + core]
         )
 
+    for i in range(PLANE):
+        value = piece(i, 1 - c).astype(BF16)
+        for h in range(2):
+            pair_send[h, i] = value[:, h * CUT : (h + 1) * CUT]
     for h in range(2):
-        pair_send[h] = grads[h, 1 - c].astype(BF16)
         pair_copy(h).start()
+    for i in range(PLANE):
+        value = piece(i, c)
+        for h in range(2):
+            grads[h, i] = value[:, h * CUT : (h + 1) * CUT]
     for h in range(2):
         pair_copy(h).wait_recv()
-        plane_send[h] = (grads[h, c] + pair_recv[h].astype(F32)).astype(BF16)
+        plane_send[h] = (grads[h] + pair_recv[h].astype(F32)).astype(BF16)
 
         @pl.loop(1, PLANE)
         def _(o):
@@ -657,7 +699,7 @@
     count = (INNER + DEPTH) // DEPTH
     for i in range(count):
         for j in range(i * DEPTH // CUT, (i + 1) * DEPTH // CUT):
-            piece = pieces[j % 2, j // 2 // PLANE, j // 2 % PLANE]
+            piece = pieces[j % 2, j // 2 % 2, j // 4]
             whole[:, pl.ds(j * CUT, CUT)] = piece.astype(F32)
         out(i).start()
     for i in range(count):
@@ -700,16 +742,19 @@
             pltpu.SMEM((1,), F32),
             pltpu.VMEM((2, Z, Y, ROWS, PC), BF16),
             pltpu.VMEM((2, Z, Y, ROWS, QC), BF16),
-            pltpu.VMEM((TEXTS, E), BF16),
-            pltpu.VMEM((X, 2 * ROWS, E // 2), BF16),
+            pltpu.VMEM((2 * TEXTS, E), BF16),
+            pltpu.VMEM((2, X, 2 * ROWS, E // 2), BF16),
             pltpu.VMEM((IMAGES, E), BF16),
             pltpu.VMEM((IMAGES, E), F32),
+            pltpu.VMEM((X, 2 * ROWS, E // 2), BF16),
+            pltpu.VMEM((X, 2 * ROWS, E // 2), BF16),
             pltpu.VMEM((X - 1, 2 * ROWS, E // 2), BF16),
             pltpu.VMEM((X, 2 * ROWS, E // 2), BF16),
             pltpu.VMEM((ROWS, E), F32),
             pltpu.VMEM((ROWS, E), F32),
             pltpu.VMEM((ROWS, DEPTH), F32),
-            pltpu.VMEM((2, 2, PLANE, RANK, CUT), F32),
+            pltpu.VMEM((ROWS, DEPTH), BF16),
+            pltpu.VMEM((2, PLANE, RANK, CUT), F32),
             pltpu.VMEM((2, PLANE, RANK, CUT), BF16),
             pltpu.VMEM((2, PLANE, RANK, CUT), BF16),
             pltpu.VMEM((2, PLANE, RANK, CUT), BF16),
@@ -717,21 +762,23 @@
             pltpu.VMEM((2, Z, RANK, CUT), BF16),
             pltpu.VMEM((2, 2, PLANE, RANK, CUT), BF16),
             dma((10,)),
-            dma((UP + DOWN,)),
+            dma((2 * HOPS,)),
             dma((Z,)),
-            dma((Z, 2)),
-            dma((Z, 2)),
+            dma((2,)),
+            dma((2,)),
+            dma((Z, 3)),
+            dma((Z, 3)),
             dma((Z, 2)),
             dma((Z, 2)),
             dma((Y - 1,)),
             dma((Y,)),
-            dma((UP + DOWN, Y)),
+            dma((2 * HOPS + 2, Y)),
             dma((Z, Y)),
-            dma((Z,)),
-            dma((Z,)),
-            dma((Z,)),
-            dma((Z,)),
             dma((X - 1,)),
+            dma((X,)),
+            dma((X,)),
+            dma((X,)),
+            dma((X,)),
             dma((X,)),
             dma((X - 1,)),
             dma((X,)),

time: 79.4 us -> 77.1 us (0.971)
  Pallas kernels: 77.4 us -> 75.1 us
    pallas_call x1, Pallas kernels: 75.1 us -> 72.8 us  [body(): pl.pallas_call(kernel, out_shape=(jax.ShapeDtypeStruct((ROWS, E), F32), j...]
where the time goes in v4:
time: 77.1 us; the launch traced here: 77 us
  Pallas kernels  75.1 us (97%)
  between operations  1.93 us (3%)
    pallas_call x1, Pallas kernels, body(): pl.pallas_call(kernel, out_shape=(jax.ShapeDtypeStruct((ROWS, E), F32), j...  72.8 us
    pallas_call x1, Pallas kernels, body(): pl.pallas_call(finish, out_shape=(jax.ShapeDtypeStruct((ROWS, E), F32), j...  2.25 us

profile of v4, /device:TPU:1, one launch (start us, length us, event | category | flops | bytes accessed | tf_op | source)
XLA Modules:
  0.0 77.0 jit_solution(2350712862358178641)
XLA Ops:
  1.9 72.8 %shard_map.121 = (f32[56,1024]{1,0:T(8,128)}, bf16[2,2,16,16,256]{4,3,2,1,0:T(8,128)(2,1)}) custom-call(bf16[56,12288]{1,0:T(8,128)(2,1)} %inner_h.1, bf16[56,3072]{1,0:T(8,128)(2,1)} %trunk_h.1, bf16[16,12288]{1,0:T(8,128)(2,1)} %bitcast.4, bf16[16,3072]{1,0:T(8,128)(2,1)} %widen_h.1, f32[1,3072]{1,0:T(1,128)} %bitcast.5, f32[1,3072]{1,0:T(1,128)} %bitcast.6, ...), custom_call_target="tpu_custom_call" | custom-call | tf_op jit(solution)/shard_map/pallas_call | solution.py:724
  74.8 2.2 %shard_map.122 = (f32[56,1024]{1,0:T(8,128)}, f32[16,12288]{1,0:T(8,128)}, f32[16,3072]{1,0:T(8,128)}) custom-call(f32[56,1024]{1,0:T(8,128)} %get-tuple-element.8.dv_h, bf16[2,2,16,16,256]{4,3,2,1,0:T(8,128)(2,1)} %get-tuple-element.9.grad_h), custom_call_target="tpu_custom_call" | custom-call | tf_op jit(solution)/shard_map/pallas_call | solution.py:812

commit v5 on v4

--- a/solution.py
+++ b/solution.py
@@ -20,8 +20,9 @@
 IMAGES = 2 * SIDE
 TEXTS = Y * ROWS
 PLANE = X * Y
-CUT = 256
-WIDE = 2 * CUT
+WIDE = 512
+PARTS = 2
+CUT = WIDE // PARTS
 HOPS = Z // 2 - 1
 
 
@@ -252,7 +253,7 @@
     p_up(z, 0).start()
     p_down(z, 0).start()
     p_spread(z, False)
-    for o in (1, 3, 2):
+    for o in (2, 1, 3):
         q_y(o).start()
     q_up(z, 0, 0).start()
     q_down(z, 0, 0).start()
@@ -413,6 +414,9 @@
         remote(ref, ref, img_send.at[0], img_recv.at[at_x(o)], sibling).wait_recv()
         images_over(at_x(o)).start()
 
+    p_ring(4)
+    p_pass(3)
+
     @pl.loop(0, X)
     def _(xx):
         ref = image_wire.at[1 - c, xx]
@@ -428,42 +432,34 @@
     shift = jnp.full((1, 2 * TEXTS), shift_s[0], F32)
     dv[...] = jnp.zeros_like(dv)
 
-    @pl.loop(0, Z // 2 + 1)
+    q_ring(3, rest)
+
+    def fill(i, zz):
+        part = pl.ds(i * TEXTS, TEXTS)
+        tile[part, :PC] = tp[c, zz].astype(F32).reshape(TEXTS, PC).astype(BF16)
+        tile[part, PC:] = tq[c, zz].astype(F32).reshape(TEXTS, QC).astype(BF16)
+
+    @pl.loop(0, Z // 2)
     def _(s):
         @pl.when(s == 1)
         def _():
-            p_ring(4)
-            p_pass(3)
             p_end(1)
 
         @pl.when(s == 2)
         def _():
-            q_ring(3, rest)
             p_end(2)
 
         @pl.when(s == 3)
         def _():
             p_end(3)
 
-        @pl.when(s == 4)
-        def _():
-            q_ring(4, own + rest)
-            p_pass(4)
-            p_end(4)
-
-        def fill(i, zz):
-            part = pl.ds(i * TEXTS, TEXTS)
-            tile[part, :PC] = tp[c, zz].astype(F32).reshape(TEXTS, PC).astype(BF16)
-            tile[part, PC:] = tq[c, zz].astype(F32).reshape(TEXTS, QC).astype(BF16)
-
         fill(0, at_z(-s))
-        single = (s == 0) | (s == Z // 2)
-
-        @pl.when(single)
+
+        @pl.when(s == 0)
         def _():
             tile[pl.ds(TEXTS, TEXTS)] = jnp.zeros((TEXTS, E), BF16)
 
-        @pl.when(jnp.logical_not(single))
+        @pl.when(s > 0)
         def _():
             fill(1, at_z(s))
 
@@ -491,10 +487,21 @@
     def rows_of(core, xx):
         return pl.ds(pl.multiple_of((core * X + xx) * ROWS, 8), ROWS)
 
-    order = (*range(1, X), 0)
-    for o in order:
-        to_wire(cross_send.at[o], dv[rows_of(1 - c, at_x(o))])
-        cross(o).start()
+    order = (2, 1, 3, 0)
+    q_ring(4, own + rest)
+    p_pass(4)
+    p_end(4)
+    fill(0, at_z(Z // 2))
+    last = pl.ds(0, TEXTS)
+    for core in (1 - c, c):
+        rows = pl.ds(pl.multiple_of(core * SIDE, SIDE), SIDE)
+        cosine = nt(images[rows], tile[last])
+        weights = sharp[:, :TEXTS] * jax.nn.sigmoid(sharp[:, :TEXTS] * cosine + shift[:, :TEXTS])
+        dv[rows] += nn(weights.astype(BF16), tile[last])
+        if core is not c:
+            for o in order:
+                to_wire(cross_send.at[o], dv[rows_of(1 - c, at_x(o))])
+                cross(o).start()
     for o in order:
         cross(o).wait_recv()
         derivative = dv[rows_of(c, at_x(o))] + from_wire(cross_recv.at[o])
@@ -509,7 +516,7 @@
             if o > 0:
                 send_sum(o).wait_send()
 
-    for o in range(1, X):
+    for o in (1, 3, 2):
         ref = dv_recv.at[at_x(o)]
         remote(ref, ref, rs_send.at[0], rs_recv.at[at_x(o)], sibling).wait_recv()
         derivative = derivative + from_wire(ref)
@@ -593,15 +600,15 @@
 
     for i in range(PLANE):
         value = piece(i, 1 - c).astype(BF16)
-        for h in range(2):
+        for h in range(PARTS):
             pair_send[h, i] = value[:, h * CUT : (h + 1) * CUT]
-    for h in range(2):
+    for h in range(PARTS):
         pair_copy(h).start()
     for i in range(PLANE):
         value = piece(i, c)
-        for h in range(2):
+        for h in range(PARTS):
             grads[h, i] = value[:, h * CUT : (h + 1) * CUT]
-    for h in range(2):
+    for h in range(PARTS):
         pair_copy(h).wait_recv()
         plane_send[h] = (grads[h] + pair_recv[h].astype(F32)).astype(BF16)
 
@@ -610,7 +617,7 @@
             plane_copy(h, o).start()
 
         plane_recv[h, k] = plane_send[h, k]
-    for h in range(2):
+    for h in range(PARTS):
 
         @pl.loop(1, PLANE)
         def _(o):
@@ -622,7 +629,7 @@
         def _(o):
             ring_copy(h, o).start()
 
-    for h in range(2):
+    for h in range(PARTS):
 
         @pl.loop(1, Z)
         def _(o):
@@ -635,7 +642,7 @@
             back_copy(h, o).start()
 
         last_copy(h, k).start()
-    for h in range(2):
+    for h in range(PARTS):
 
         @pl.loop(1, PLANE)
         def _(o):
@@ -643,7 +650,7 @@
             last_copy(h, at_k(o)).start()
 
         out_copy(h, c).start()
-    for h in range(2):
+    for h in range(PARTS):
 
         @pl.loop(0, PLANE)
         def _(kk):
@@ -653,7 +660,7 @@
 
     @pending.append
     def _():
-        for h in range(2):
+        for h in range(PARTS):
             pair_copy(h).wait_send()
 
             @pl.loop(1, PLANE)
@@ -699,7 +706,8 @@
     count = (INNER + DEPTH) // DEPTH
     for i in range(count):
         for j in range(i * DEPTH // CUT, (i + 1) * DEPTH // CUT):
-            piece = pieces[j % 2, j // 2 % 2, j // 4]
+            wide = j // PARTS
+            piece = pieces[j % PARTS, wide % 2, wide // 2]
             whole[:, pl.ds(j * CUT, CUT)] = piece.astype(F32)
         out(i).start()
     for i in range(count):
@@ -725,7 +733,7 @@
         kernel,
         out_shape=(
             jax.ShapeDtypeStruct((ROWS, E), F32),
-            jax.ShapeDtypeStruct((2, 2, PLANE, RANK, CUT), BF16),
+            jax.ShapeDtypeStruct((PARTS, 2, PLANE, RANK, CUT), BF16),
         ),
         in_specs=[anywhere] * 8 + [pl.BlockSpec(memory_space=pltpu.HBM)] * 2,
         out_specs=(anywhere, anywhere),
@@ -754,13 +762,13 @@
             pltpu.VMEM((ROWS, E), F32),
             pltpu.VMEM((ROWS, DEPTH), F32),
             pltpu.VMEM((ROWS, DEPTH), BF16),
-            pltpu.VMEM((2, PLANE, RANK, CUT), F32),
-            pltpu.VMEM((2, PLANE, RANK, CUT), BF16),
-            pltpu.VMEM((2, PLANE, RANK, CUT), BF16),
-            pltpu.VMEM((2, PLANE, RANK, CUT), BF16),
-            pltpu.VMEM((2, PLANE, RANK, CUT), BF16),
-            pltpu.VMEM((2, Z, RANK, CUT), BF16),
-            pltpu.VMEM((2, 2, PLANE, RANK, CUT), BF16),
+            pltpu.VMEM((PARTS, PLANE, RANK, CUT), F32),
+            pltpu.VMEM((PARTS, PLANE, RANK, CUT), BF16),
+            pltpu.VMEM((PARTS, PLANE, RANK, CUT), BF16),
+            pltpu.VMEM((PARTS, PLANE, RANK, CUT), BF16),
+            pltpu.VMEM((PARTS, PLANE, RANK, CUT), BF16),
+            pltpu.VMEM((PARTS, Z, RANK, CUT), BF16),
+            pltpu.VMEM((PARTS, 2, PLANE, RANK, CUT), BF16),
             dma((10,)),
             dma((2 * HOPS,)),
             dma((Z,)),
@@ -782,17 +790,17 @@
             dma((X,)),
             dma((X - 1,)),
             dma((X,)),
-            dma((2,)),
-            dma((2,)),
-            dma((2, PLANE - 1)),
-            dma((2, PLANE)),
-            dma((2, Z - 1)),
-            dma((2, Z)),
-            dma((2, PLANE - 1)),
-            dma((2, PLANE)),
-            dma((2, PLANE)),
-            dma((2, PLANE)),
-            dma((5,)),
+            dma((PARTS,)),
+            dma((PARTS,)),
+            dma((PARTS, PLANE - 1)),
+            dma((PARTS, PLANE)),
+            dma((PARTS, Z - 1)),
+            dma((PARTS, Z)),
+            dma((PARTS, PLANE - 1)),
+            dma((PARTS, PLANE)),
+            dma((PARTS, PLANE)),
+            dma((PARTS, PLANE)),
+            dma((1 + 2 * PARTS,)),
         ],
         compiler_params=pltpu.CompilerParams(
             collective_id=0, has_side_effects=True, vmem_limit_bytes=64_800_000
@@ -820,7 +828,7 @@
         out_specs=(anywhere,) * 3,
         scratch_shapes=[
             pltpu.VMEM((ROWS, E), F32),
-            pltpu.VMEM((2, 2, PLANE, RANK, CUT), BF16),
+            pltpu.VMEM((PARTS, 2, PLANE, RANK, CUT), BF16),
             pltpu.VMEM((RANK, INNER + DEPTH), F32),
             dma((2,)),
             dma,

time: 77.1 us -> 76.5 us (level)
  no operation moved by 1% of the time
where the time goes in v5:
time: 76.5 us; the launch traced here: 76.3 us
  Pallas kernels  74.4 us (97%)
  between operations  1.93 us (3%)
    pallas_call x1, Pallas kernels, body(): pl.pallas_call(kernel, out_shape=(jax.ShapeDtypeStruct((ROWS, E), F32), j...  72.2 us
    pallas_call x1, Pallas kernels, body(): pl.pallas_call(finish, out_shape=(jax.ShapeDtypeStruct((ROWS, E), F32), j...  2.25 us

profile of v5, /device:TPU:1, one launch (start us, length us, event | category | flops | bytes accessed | tf_op | source)
XLA Modules:
  0.0 76.3 jit_solution(18193524271350749427)
XLA Ops:
  1.9 72.2 %shard_map.121 = (f32[56,1024]{1,0:T(8,128)}, bf16[2,2,16,16,256]{4,3,2,1,0:T(8,128)(2,1)}) custom-call(bf16[56,12288]{1,0:T(8,128)(2,1)} %inner_h.1, bf16[56,3072]{1,0:T(8,128)(2,1)} %trunk_h.1, bf16[16,12288]{1,0:T(8,128)(2,1)} %bitcast.4, bf16[16,3072]{1,0:T(8,128)(2,1)} %widen_h.1, f32[1,3072]{1,0:T(1,128)} %bitcast.5, f32[1,3072]{1,0:T(1,128)} %bitcast.6, ...), custom_call_target="tpu_custom_call" | custom-call | tf_op jit(solution)/shard_map/pallas_call | solution.py:732
  74.1 2.2 %shard_map.122 = (f32[56,1024]{1,0:T(8,128)}, f32[16,12288]{1,0:T(8,128)}, f32[16,3072]{1,0:T(8,128)}) custom-call(f32[56,1024]{1,0:T(8,128)} %get-tuple-element.8.dv_h, bf16[2,2,16,16,256]{4,3,2,1,0:T(8,128)(2,1)} %get-tuple-element.9.grad_h), custom_call_target="tpu_custom_call" | custom-call | tf_op jit(solution)/shard_map/pallas_call | solution.py:820

commit v6 on v5

--- a/solution.py
+++ b/solution.py
@@ -686,16 +686,19 @@
 def finish(
     dv_h, grad_h, dv_out, down_out, up_out, dv, pieces, whole, in_sem, dv_sem, down_sem, up_sem
 ):
-    reads = [
-        pltpu.make_async_copy(dv_h, dv, in_sem.at[0]),
-        pltpu.make_async_copy(grad_h, pieces, in_sem.at[1]),
-    ]
-    for read in reads:
-        read.start()
-    for read in reads:
-        read.wait()
-    dv_copy = pltpu.make_async_copy(dv, dv_out, dv_sem)
-    dv_copy.start()
+    count = (INNER + DEPTH) // DEPTH
+    slots = DEPTH // WIDE // 2
+
+    def read(i):
+        part = pl.ds(i * slots, slots)
+        return pltpu.make_async_copy(
+            grad_h.at[:, :, part], pieces.at[:, :, part], in_sem.at[1 + i]
+        )
+
+    dv_read = pltpu.make_async_copy(dv_h, dv, in_sem.at[0])
+    for i in range(count):
+        read(i).start()
+    dv_read.start()
 
     def out(i):
         if i < INNER // DEPTH:
@@ -703,13 +706,16 @@
             return pltpu.make_async_copy(whole.at[:, cols], down_out.at[:, cols], down_sem.at[i])
         return pltpu.make_async_copy(whole.at[:, pl.ds(INNER, DEPTH)], up_out, up_sem)
 
-    count = (INNER + DEPTH) // DEPTH
     for i in range(count):
+        read(i).wait()
         for j in range(i * DEPTH // CUT, (i + 1) * DEPTH // CUT):
             wide = j // PARTS
             piece = pieces[j % PARTS, wide % 2, wide // 2]
             whole[:, pl.ds(j * CUT, CUT)] = piece.astype(F32)
         out(i).start()
+    dv_read.wait()
+    dv_copy = pltpu.make_async_copy(dv, dv_out, dv_sem)
+    dv_copy.start()
     for i in range(count):
         out(i).wait()
     dv_copy.wait()
@@ -830,7 +836,7 @@
             pltpu.VMEM((ROWS, E), F32),
             pltpu.VMEM((PARTS, 2, PLANE, RANK, CUT), BF16),
             pltpu.VMEM((RANK, INNER + DEPTH), F32),
-            dma((2,)),
+            dma((1 + (INNER + DEPTH) // DEPTH,)),
             dma,
             dma((INNER // DEPTH,)),
             dma,

time: 76.5 us -> 76.2 us (level)
  no operation moved by 1% of the time
where the time goes in v6:
time: 76.2 us; the launch traced here: 76.1 us
  Pallas kernels  74.2 us (97%)
  between operations  1.93 us (3%)
    pallas_call x1, Pallas kernels, body(): pl.pallas_call(kernel, out_shape=(jax.ShapeDtypeStruct((ROWS, E), F32), j...  72.2 us
    pallas_call x1, Pallas kernels, body(): pl.pallas_call(finish, out_shape=(jax.ShapeDtypeStruct((ROWS, E), F32), j...  2.02 us

profile of v6, /device:TPU:1, one launch (start us, length us, event | category | flops | bytes accessed | tf_op | source)
XLA Modules:
  0.0 76.1 jit_solution(8724464280444075209)
XLA Ops:
  1.9 72.2 %shard_map.121 = (f32[56,1024]{1,0:T(8,128)}, bf16[2,2,16,16,256]{4,3,2,1,0:T(8,128)(2,1)}) custom-call(bf16[56,12288]{1,0:T(8,128)(2,1)} %inner_h.1, bf16[56,3072]{1,0:T(8,128)(2,1)} %trunk_h.1, bf16[16,12288]{1,0:T(8,128)(2,1)} %bitcast.4, bf16[16,3072]{1,0:T(8,128)(2,1)} %widen_h.1, f32[1,3072]{1,0:T(1,128)} %bitcast.5, f32[1,3072]{1,0:T(1,128)} %bitcast.6, ...), custom_call_target="tpu_custom_call" | custom-call | tf_op jit(solution)/shard_map/pallas_call | solution.py:738
  74.1 2.0 %shard_map.122 = (f32[56,1024]{1,0:T(8,128)}, f32[16,12288]{1,0:T(8,128)}, f32[16,3072]{1,0:T(8,128)}) custom-call(f32[56,1024]{1,0:T(8,128)} %get-tuple-element.8.dv_h, bf16[2,2,16,16,256]{4,3,2,1,0:T(8,128)(2,1)} %get-tuple-element.9.grad_h), custom_call_target="tpu_custom_call" | custom-call | tf_op jit(solution)/shard_map/pallas_call | solution.py:826
